TPU v7x, 512 devices: a whole 4x8x8 slice. The times are simulated.
512 devices in a mesh: dp: 64 (over x, z_lo, y), mp: 8 (over z_hi, core).
Axes of the slice: x: 4, y: 8, z: 8 (z_hi: 4, z_lo: 2; z = z_hi * 2 + z_lo), core: 2. Of those that a mesh axis runs over, the one named last changes fastest.
Arguments:
- tokens: bfloat16 [81920, 5120], P('dp', 'mp')
- key_weight: bfloat16 [512, 5120], P(None, 'mp'), may hold values from -0.078125 to 0.078125
- key_gain: float32 [512], replicated, may hold values from 0.1 to 1.9
- cotangent: bfloat16 [81920, 512], P('dp', 'mp'), may hold values from -6 to 6
- momentum: bfloat16 [64, 512, 5120], P('dp', None, 'mp')
- band_row: int32 [8, 80], P(None, 'mp'), may hold values from 0 to 3
- band_col: int32 [8, 80], P(None, 'mp'), may hold values from 0 to 3
Outputs:
- update: bfloat16 [512, 5120], P(None, 'mp')
- new_momentum: bfloat16 [64, 512, 5120], P('dp', None, 'mp')
Inputs may be any that keep to these rules, and one draw needn't show every extreme that they name: band_row and band_col are the same on every replica; the transform's bands stand at low frequencies.
All inputs are finite; a program needn't handle non-finite values.
Results may differ from a plain program's by a relative error of at most 0.0075.
Values may be sent and summed in bfloat16 or wider, within the bound.
A program may use at most 64 MiB of HBM per device.

v0:
```python
import math

import jax
import jax.numpy as jnp
from jax import lax
from jax.sharding import PartitionSpec as P

SPAN = 64
BAND = 8
BANDS = 8


EPS = 1e-06
DECAY = 0.9


def dct_table():
    frequency = jnp.arange(SPAN, dtype=jnp.float32)[:, None]
    position = jnp.arange(SPAN, dtype=jnp.float32)[None, :]
    cosines = jnp.cos(jnp.pi * (2.0 * position + 1.0) * frequency / (2.0 * SPAN))
    row_norms = jnp.where(frequency == 0, jnp.sqrt(1.0 / SPAN), jnp.sqrt(2.0 / SPAN))
    return cosines * row_norms


def select_basis(band_index, band_basis):
    picked = (band_index[..., None] == jnp.arange(BANDS, dtype=jnp.int32)).astype(jnp.float32)
    return jnp.einsum("rcb,bkn->rckn", picked, band_basis, precision=lax.Precision.HIGHEST)


def band_coeffs(blocks, row_basis, col_basis):
    first_section = jnp.einsum(
        "rckn,rncp->rckp", row_basis, blocks, precision=lax.Precision.HIGHEST
    )
    return jnp.einsum("rckp,rclp->rckl", first_section, col_basis, precision=lax.Precision.HIGHEST)


def band_rebuild(coeffs, row_basis, col_basis):
    first_section = jnp.einsum(
        "rckl,rclp->rckp", coeffs, col_basis, precision=lax.Precision.HIGHEST
    )
    return jnp.einsum("rckn,rckp->rncp", row_basis, first_section, precision=lax.Precision.HIGHEST)


def on_device(tokens, key_weight, key_gain, cotangent, momentum, band_row, band_col):
    width_kv = key_weight.shape[0]
    tok_rows = tokens.shape[0]
    partial_value = lax.dot_general(
        tokens, key_weight, (((1,), (1,)), ((), ())), preferred_element_type=jnp.float32
    )
    key_rows = lax.psum(partial_value.astype(jnp.bfloat16), "mp").astype(jnp.float32)
    cot_rows = lax.all_gather(cotangent, "mp", axis=1, tiled=True).astype(jnp.float32)
    inverse = lax.rsqrt(jnp.mean(key_rows * key_rows, axis=-1, keepdims=True) + EPS)
    scaled = key_gain * cot_rows
    inner_sum = jnp.sum(scaled * key_rows, axis=-1, keepdims=True)
    dkeys = (inverse * scaled - inverse**3 * key_rows * inner_sum / width_kv).astype(jnp.bfloat16)
    gradient = lax.dot_general(
        dkeys, tokens, (((0,), (0,)), ((), ())), preferred_element_type=jnp.float32
    ) / math.sqrt(tok_rows)
    momentum_new = DECAY * momentum[0].astype(jnp.float32) + gradient
    band_basis = dct_table().reshape(BANDS, BAND, SPAN)
    row_basis = select_basis(band_row, band_basis)
    col_basis = select_basis(band_col, band_basis)
    rows_blk = width_kv // SPAN
    cols_blk = momentum_new.shape[1] // SPAN
    blocks = momentum_new.reshape(rows_blk, SPAN, cols_blk, SPAN)
    coeffs = band_coeffs(blocks, row_basis, col_basis)
    own_part = band_rebuild(coeffs, row_basis, col_basis).reshape(width_kv, cols_blk * SPAN)
    new_momentum = (momentum_new - own_part).astype(jnp.bfloat16)[None]
    flattened = coeffs.reshape(rows_blk, cols_blk * BAND * BAND)
    everyone = lax.all_gather(flattened[None], "dp", axis=0, tiled=True)
    summed = jnp.sum(everyone, axis=0)
    averaged = summed.reshape(coeffs.shape) / lax.axis_size("dp")
    update = (
        band_rebuild(averaged, row_basis, col_basis)
        .reshape(width_kv, cols_blk * SPAN)
        .astype(jnp.bfloat16)
    )
    return (update, new_momentum)


def solution(mesh):
    return jax.shard_map(
        on_device,
        mesh=mesh,
        in_specs=(
            P("dp", "mp"),
            P(None, "mp"),
            P(),
            P("dp", "mp"),
            P("dp", None, "mp"),
            P(None, "mp"),
            P(None, "mp"),
        ),
        out_specs=(P(None, "mp"), P("dp", None, "mp")),
        check_vma=False,
    )
```

profile of v0, /device:TPU:128, one launch (start us, length us, event | category | flops | bytes accessed | tf_op | source)
XLA Modules:
  0.0 470.6 jit_solution(8125810739028951988)
XLA Ops:
  7.2 0.0 copy-start
  7.2 0.0 all-gather.3.cloned.1.call-start
  7.2 0.7 all-gather.3.cloned.1.call-update
  7.9 0.0 copy-start.5
  7.9 0.0 all-reduce.2.cloned.1.call-start
  8.0 0.6 copy-done
  8.6 3.4 convolution_convert_fusion
  12.0 0.0 copy-start.6
  12.0 0.0 all-reduce.2.cloned.1.call-update
  12.0 0.0 all-gather.5.cloned.1.call-start
  12.1 0.0 copy-done.5
  12.1 1.3 fusion.26
  13.4 0.0 copy-done.6
  13.4 0.0 copy-start.7
  13.4 0.5 fusion.28
  13.9 33.0 %all-gather.3.cloned.1.call-done = bf16[1280,512]{0,1:T(8,128)(2,1)} async-done(((bf16[1280,64]{0,1:T(8,128)(2,1)}), bf16[1280,512]{0,1:T(8,128)(2,1)}) %all-gather.3.cloned.1.call-update) | async-done | bytes 1310736 | tf_op jit(solution)/shard_map/all_gather | solution.py:51
  46.9 1.6 copy.23
  48.5 0.0 copy-start.1
  48.6 82.9 %all-reduce.2.cloned.1.call-done = bf16[1280,512]{1,0:T(8,128)(2,1)} async-done(((bf16[1280,512]{1,0:T(8,128)(2,1)}), bf16[1280,512]{1,0:T(8,128)(2,1)}) %all-reduce.2.cloned.1.call-update) | async-done | bytes 1310736 | tf_op jit(solution)/shard_map/psum | solution.py:50
  131.4 0.0 copy-done.7
  131.4 0.0 copy-start.4
  131.4 0.0 copy-start.8
  131.5 2.1 fusion
  133.6 0.0 copy-done.1
  133.6 0.0 copy-done.4
  133.6 0.0 copy-done.8
  133.6 3.0 fusion.9
  136.7 2.4 reshape.77
  139.1 0.0 copy-start.2
  139.1 5.0 %fusion.6 = f32[8,10,8,64]{3,2,1,0:T(8,128)S(1)} fusion(f32[8,64,10,64]{3,2,1,0:T(8,128)} %reshape.77, f32[8,10,8,64]{3,1,2,0:T(8,128)S(1)} %fusion.28), kind=kOutput, calls=%fused_computation.10 | convolution fusion | flops 31457280 | bytes 1638400 | tf_op jit(solution)/shard_map/rckn,rncp->rckp/dot_general | solution.py:31
  144.1 0.0 copy-done.2
  144.1 1.4 fusion.21
  145.6 1.7 broadcast_in_dim_reshape.3
  147.3 0.0 all-gather.5.cloned.1.call-update
  147.3 1.8 fusion.17
  149.2 5.8 %convolution_bitcast_fusion = f32[8,64,10,64]{1,3,2,0:T(8,128)} fusion(f32[8,10,8,64]{3,2,1,0:T(8,128)S(1)} %fusion.17, f32[8,10,8,64]{3,1,2,0:T(8,128)S(1)} %fusion.28), kind=kOutput, calls=%fused_computation.13 | convolution fusion | flops 31457280 | bytes 1638400 | tf_op jit(solution)/shard_map/rckn,rckp->rncp/dot_general | solution.py:41
  155.0 5.0 %copy.41 = f32[8,64,10,64]{3,2,1,0:T(8,128)} copy(f32[8,64,10,64]{1,3,2,0:T(8,128)} %convolution_bitcast_fusion) | data formatting | bytes 2621440 | tf_op jit(solution)/shard_map/reshape | solution.py:67
  160.0 4.2 reshape.79
  164.1 2.3 fusion.16
  166.4 0.0 copy-start.3
  166.4 283.9 %all-gather.5.cloned.1.call-done = f32[64,8,640]{2,1,0:T(8,128)} async-done(((f32[1,8,640]{2,1,0:T(8,128)}), f32[64,8,640]{2,1,0:T(8,128)}) %all-gather.5.cloned.1.call-update) | async-done | bytes 1310736 | tf_op jit(solution)/shard_map/all_gather | solution.py:70
  450.3 1.4 reduce_sum.29
  451.7 0.2 div.44
  451.9 0.0 copy-done.3
  451.9 0.7 fusion.19
  452.6 4.3 fusion.8
  456.9 3.5 copy.40
  460.4 3.7 reshape.78
  (4 shorter events, 0.0 us)
Async XLA Ops:
  7.2 1.4 copy-start
  7.2 39.8 %all-gather.3.cloned.1.call-start = ((), (), s32[]{:S(2)}) async-start(), calls=%async_computation.1 | async-start | bytes 1474560 | tf_op jit(solution)/shard_map/all_gather | solution.py:51
  7.9 4.2 copy-start.5
  7.9 123.5 %all-reduce.2.cloned.1.call-start = ((), (), s32[]{:S(2)}) async-start(), calls=%async_computation | async-start | bytes 2621440 | tf_op jit(solution)/shard_map/psum | solution.py:50
  12.0 1.4 copy-start.6
  12.0 438.3 %all-gather.5.cloned.1.call-start = ((), (), s32[]{:S(2)}) async-start(), calls=%async_computation.2 | async-start | bytes 1331200 | tf_op jit(solution)/shard_map/all_gather | solution.py:70
  13.4 118.1 %copy-start.7 = (f32[512]{0:T(512)S(1)}, f32[512]{0:T(512)}, u32[]{:S(2)}) copy-start(f32[512]{0:T(512)} %param.9) | copy-start | bytes 6148
  48.5 85.1 %copy-start.1 = (bf16[1280,512]{1,0:T(8,128)(2,1)}, bf16[1280,512]{1,0:T(8,128)(2,1)S(1)}, u32[]{:S(2)}) copy-start(bf16[1280,512]{1,0:T(8,128)(2,1)S(1)} %copy.23) | copy-start | bytes 3932164
  131.4 2.2 copy-start.4
  131.4 2.2 copy-start.8
  139.1 5.0 %copy-start.2 = (f32[8,10,8,64]{3,1,2,0:T(8,128)S(1)}, f32[8,10,8,64]{3,1,2,0:T(8,128)}, u32[]{:S(2)}) copy-start(f32[8,10,8,64]{3,1,2,0:T(8,128)} %fusion.26) | copy-start | bytes 491524
  166.4 285.5 %copy-start.3 = (f32[8,10,8,64]{3,1,2,0:T(8,128)S(1)}, f32[8,10,8,64]{3,1,2,0:T(8,128)}, u32[]{:S(2)}) copy-start(f32[8,10,8,64]{3,1,2,0:T(8,128)} %fusion.26) | copy-start | bytes 491524
Sparse Core Ops, SparseCore 0:
  10.1 36.7 all-gather.2
  49.9 81.5 all-reduce.1
  147.5 302.7 all-gather.4
where the time goes:
time: 472 us; the launch traced here: 471 us
  waiting for transfers between devices  401 us (85%)
  matrix products  27.3 us (6%)
  local copies, waits for them, and re-layouts  23 us (5%)
  between operations  13.9 us (3%)
  other arithmetic  5.87 us (1%)
    all_gather x1, waiting for transfers between devices, on_device(): everyone = lax.all_gather(flattened[None], 'dp', axis=0, tiled=True)  284 us
    psum x1, waiting for transfers between devices, on_device(): lax.psum(partial_value.astype(jnp.bfloat16), 'mp').astype(jnp.float32)  82.9 us
    all_gather x1, waiting for transfers between devices, on_device(): lax.all_gather(cotangent, 'mp', axis=1, tiled=True).astype(jnp.float32)  33 us
    dot_general x2, matrix products, band_rebuild(): jnp.einsum('rckn,rckp->rncp', row_basis, first_section, precision=lax.Pre...  10.1 us
  transfers between devices with their start and end apart: 3, of which 3 were waited for; matrix products, arithmetic and copies ran while one was open for 5% of the time, Pallas kernels for 0%

commit v1 on v0

v1 whole, which is shorter than its diff:
```python
import math

import jax
import jax.numpy as jnp
import ml_dtypes
import numpy as np
from jax import lax
from jax.experimental import pallas as pl
from jax.experimental.pallas import tpu as pltpu
from jax.sharding import PartitionSpec as P

MESH = pl.DeviceIdType.MESH
BF = jnp.bfloat16
F32 = jnp.float32

SPAN = 64
BAND = 8
OFFSETS = 4
LOW = BAND * OFFSETS
EPS = 1e-06
DECAY = 0.9

NY = 8
NXZ = 8
NZ = 4
N_DP = NY * NXZ
OWN = 160
KV = 512
WIDTH = 640
ROWS_BLK = KV // SPAN
COLS_BLK = WIDTH // SPAN
LANES = 128
CHUNKS = ((0, 80), (80, 80))


def split_const(table):
    high = table.astype(np.float32).astype(ml_dtypes.bfloat16)
    low = (table - high.astype(np.float64)).astype(np.float32).astype(ml_dtypes.bfloat16)
    return high, low


def tables():
    f = np.arange(SPAN, dtype=np.float64)[:, None]
    n = np.arange(SPAN, dtype=np.float64)[None, :]
    c = np.cos(np.pi * (2.0 * n + 1.0) * f / (2.0 * SPAN))
    c = c * np.where(f == 0, np.sqrt(1.0 / SPAN), np.sqrt(2.0 / SPAN))
    c = c[:LOW]
    left = np.kron(np.eye(4), c)
    right = np.zeros((COLS_BLK, SPAN, OFFSETS, LANES))
    for block in range(COLS_BLK):
        for band in range(OFFSETS):
            right[block, :, band, block * BAND : (block + 1) * BAND] = c[band * BAND : (band + 1) * BAND].T
    right = right.reshape(WIDTH, OFFSETS * LANES)
    lh, ll = split_const(left)
    rh, rl = split_const(right)
    return (
        np.concatenate([lh, ll], axis=0),
        np.stack([np.ascontiguousarray(lh.T), np.ascontiguousarray(ll.T)]),
        np.stack([rh, rl]),
    )


def dot(a, b, dims=((1,), (0,))):
    return lax.dot_general(a, b, (dims, ((), ())), preferred_element_type=F32)


def split(value):
    high = value.astype(BF)
    return high, (value - high.astype(F32)).astype(BF)


def kernel(
    x_hbm, w_hbm, gain_ref, cot_hbm, mom_hbm, row_ref, col_ref, left_hbm, left_t_hbm, right_hbm,
    upd_hbm, new_hbm,
    xv, wv, cotv, momv, leftv, left_tv, rightv,
    cot_sib, cot_mix, cot_all, part_out, part_own, part_in, pair, recv, dk, mom_new,
    row_mask, col_mask, band_y, band_xz, upd_v, new_v,
    load_sem, out_sem, cs_s, cs_r, cz_s, cz_r, ps_s, ps_r, rs_s, rs_r, ag_s, ag_r, fw_s, fw_r,
    y_s, y_r, xz_s, xz_r,
):
    dp = lax.axis_index("dp")
    mp = lax.axis_index("mp")
    zh = mp // 2
    core = mp % 2
    y = dp % NY
    xz = dp // NY
    sib = {"dp": dp, "mp": zh * 2 + (1 - core)}

    def z_peer(step):
        return {"dp": dp, "mp": ((zh + step) % NZ) * 2 + core}

    def y_peer(step):
        return {"dp": xz * NY + (y + step) % NY, "mp": mp}

    def xz_peer(step):
        return {"dp": ((xz + step) % NXZ) * NY + y, "mp": mp}

    barrier = pltpu.get_barrier_semaphore()
    peers = [y_peer(s) for s in (4, 3, 5, 2, 6, 1, 7)] + [xz_peer(s) for s in range(1, NXZ)]
    peers += [z_peer(s) for s in (2, 1, 3)] + [sib]
    for peer in peers:
        pl.semaphore_signal(barrier, inc=1, device_id=peer, device_id_type=MESH)

    loads = [pltpu.make_async_copy(w_hbm, wv, load_sem.at[0])]
    for k, (off, rows) in enumerate(CHUNKS):
        at = (slice(None), slice(None), pl.ds(off, rows))
        loads.append(pltpu.make_async_copy(x_hbm.at[at], xv.at[at], load_sem.at[1 + k]))
    base = 1 + len(CHUNKS)
    more = [(cot_hbm, cotv), (mom_hbm, momv), (left_hbm, leftv), (left_t_hbm, left_tv), (right_hbm, rightv)]
    for k, (src, dst) in enumerate(more):
        loads.append(pltpu.make_async_copy(src, dst, load_sem.at[base + k]))
    for load in loads:
        load.start()

    def remote(src, dst, send, recv_, peer):
        return pltpu.make_async_remote_copy(
            src_ref=src, dst_ref=dst, send_sem=send, recv_sem=recv_, device_id=peer, device_id_type=MESH
        )

    sent = []

    def start(copy):
        copy.start()
        sent.append(copy)

    loads[0].wait()
    for k, (off, rows) in enumerate(CHUNKS):
        loads[1 + k].wait()
        at = pl.ds(off, rows)
        for side, place in ((1 - core, part_out), (core, part_own)):
            x_rows = xv[:, side, at, :].reshape(NZ * rows, WIDTH)
            part = dot(x_rows, wv[...], ((1,), (1,)))
            place[:, at, :] = part.astype(BF).reshape(NZ, rows, KV)

    loads[base].wait()
    pl.semaphore_wait(barrier, len(peers))

    cot_swap = remote(cotv.at[:, 1 - core], cot_sib, cs_s, cs_r, sib)
    start(cot_swap)
    part_swaps = []
    for k, (off, rows) in enumerate(CHUNKS):
        at = (slice(None), pl.ds(off, rows))
        part_swaps.append(remote(part_out.at[at], part_in.at[at], ps_s.at[k], ps_r.at[k], sib))
        start(part_swaps[-1])

    cot_swap.wait_recv()
    feature = lax.broadcasted_iota(jnp.int32, (SPAN, LANES), 0)
    lane = lax.broadcasted_iota(jnp.int32, (SPAN, LANES), 1)
    put_own = (lane == feature + core * SPAN).astype(BF)
    put_sib = (lane == feature + (1 - core) * SPAN).astype(BF)
    mixed = dot(cotv[:, core].reshape(NZ * OWN, SPAN), put_own) + dot(cot_sib[...].reshape(NZ * OWN, SPAN), put_sib)
    cot_mix[...] = mixed.astype(BF).reshape(NZ, OWN, LANES)
    cot_all[zh] = cot_mix[zh]
    for step in (2, 1, 3):
        start(remote(
            cot_mix.at[(zh + step) % NZ], cot_all.at[zh], cz_s.at[step - 1], cz_r.at[step - 1], z_peer(step)
        ))

    for k, (off, rows) in enumerate(CHUNKS):
        at = pl.ds(off, rows)
        part_swaps[k].wait_recv()
        pair[:, at, :] = (part_own[:, at, :].astype(F32) + part_in[:, at, :].astype(F32)).astype(BF)
        for step in (2, 1, 3):
            start(remote(
                pair.at[(zh + step) % NZ, at], recv.at[step - 1, at],
                rs_s.at[k, step - 1], rs_r.at[k, step - 1], z_peer(step),
            ))

    block_r = lax.broadcasted_iota(jnp.int32, (BAND, WIDTH), 1) // SPAN
    block_c = lax.broadcasted_iota(jnp.int32, (BAND, LANES), 1) // BAND

    def spread(r, carry):
        of_row = jnp.zeros((BAND, WIDTH), jnp.int32)
        of_col = jnp.zeros((BAND, LANES), jnp.int32)
        for c in range(COLS_BLK):
            of_row = jnp.where(block_r == c, row_ref[r, c], of_row)
            of_col = jnp.where(block_c == c, col_ref[r, c], of_col)
        row_mask[r] = of_row
        col_mask[r] = of_col
        return carry

    lax.fori_loop(0, ROWS_BLK, spread, 0)
    for load in loads[base + 1 :]:
        load.wait()
    mom_new[...] = DECAY * momv[0].astype(F32)

    for step in (2, 1, 3):
        src = (zh + NZ - step) % NZ
        remote(cot_mix.at[0], cot_all.at[src], cz_s.at[step - 1], cz_r.at[step - 1], sib).wait_recv()
    gain = gain_ref[...]
    for k, (off, rows) in enumerate(CHUNKS):
        at = pl.ds(off, rows)
        keys = pair[zh, at, :].astype(F32)
        for step in (1, 3, 2):
            remote(pair.at[0, at], recv.at[step - 1, at], rs_s.at[k, step - 1], rs_r.at[k, step - 1], sib).wait_recv()
            keys = keys + recv[step - 1, at, :].astype(F32)
        scaled = gain * jnp.concatenate([cot_all[j, at, :].astype(F32) for j in range(NZ)], axis=-1)
        inverse = lax.rsqrt(jnp.mean(keys * keys, axis=-1, keepdims=True) + EPS)
        inner = jnp.sum(scaled * keys, axis=-1, keepdims=True)
        dk[mp, at, :] = (inverse * scaled - (inverse * inverse * inverse * inner / KV) * keys).astype(BF)
        for step in (2, 1, 3):
            start(remote(dk.at[mp, at], dk.at[mp, at], ag_s.at[k, step - 1], ag_r.at[k, step - 1], z_peer(step)))
        start(remote(dk.at[mp, at], dk.at[mp, at], fw_s.at[k, 0], fw_r.at[k, 0], sib))

    for k, (off, rows) in enumerate(CHUNKS):
        at = pl.ds(off, rows)
        for step in (1, 3, 2):
            src = ((zh + NZ - step) % NZ) * 2 + core
            got = dk.at[src, at]
            remote(got, got, ag_s.at[k, step - 1], ag_r.at[k, step - 1], sib).wait_recv()
            start(remote(got, got, fw_s.at[k, step], fw_r.at[k, step], sib))
        for step in (0, 1, 3, 2):
            got = dk.at[((zh + NZ - step) % NZ) * 2 + 1 - core, at]
            remote(got, got, fw_s.at[k, step], fw_r.at[k, step], sib).wait_recv()
        all_dk = dk[:, at, :].reshape(2 * NZ * rows, KV)
        all_x = xv[:, :, at, :].reshape(2 * NZ * rows, WIDTH)
        mom_new[...] += dot(all_dk, all_x, ((0,), (0,))) * (1.0 / math.sqrt(2 * NZ * OWN))

    picked = []
    for g in range(2):
        high, low = split(mom_new[g * 256 : (g + 1) * 256, :])
        both = dot(leftv[...], high)
        sect = both[:128] + both[128:] + dot(leftv[:128], low)
        sect = sect.reshape(4, OFFSETS, BAND, WIDTH)
        chosen = row_mask[g * 4 : (g + 1) * 4]
        total = jnp.zeros((4, BAND, WIDTH), F32)
        for band in range(OFFSETS):
            total = total + jnp.where(chosen == band, sect[:, band], 0.0)
        picked.append(total.reshape(32, WIDTH))
    sect = jnp.concatenate(picked, axis=0)
    high, low = split(sect)
    both = dot(jnp.concatenate([high, low], axis=0), rightv[0])
    full = both[:64] + both[64:] + dot(high, rightv[1])
    chosen = col_mask[...].reshape(64, LANES)
    coeffs = jnp.zeros((64, LANES), F32)
    for band in range(OFFSETS):
        coeffs = coeffs + jnp.where(chosen == band, full[:, band * LANES : (band + 1) * LANES], 0.0)

    band_y[y] = coeffs.astype(BF)
    for step in (4, 3, 5, 2, 6, 1, 7):
        start(remote(band_y.at[y], band_y.at[y], y_s.at[step - 1], y_r.at[step - 1], y_peer(step)))

    def rebuild(values, put):
        parts = [jnp.where(chosen == band, values, 0.0) for band in range(OFFSETS)]
        high, low = split(jnp.concatenate(parts, axis=1))
        both = dot(jnp.concatenate([high, low], axis=0), rightv[0], ((1,), (1,)))
        first = both[:64] + both[64:] + dot(high, rightv[1], ((1,), (1,)))
        for g in range(2):
            rows = first[g * 32 : (g + 1) * 32].reshape(4, 1, BAND, WIDTH)
            bands = lax.broadcasted_iota(jnp.int32, (4, OFFSETS, BAND, WIDTH), 1)
            mask = row_mask[g * 4 : (g + 1) * 4].reshape(4, 1, BAND, WIDTH)
            spread_rows = jnp.where(mask == bands, rows, 0.0).reshape(128, WIDTH)
            high, low = split(spread_rows)
            out = dot(left_tv[0], high) + dot(left_tv[1], high) + dot(left_tv[0], low)
            put(g, out)

    def put_new(g, own):
        at = slice(g * 256, (g + 1) * 256)
        new_v[0, at, :] = (mom_new[at, :] - own).astype(BF)

    rebuild(coeffs, put_new)
    store_new = pltpu.make_async_copy(new_v, new_hbm, out_sem.at[0])
    store_new.start()

    for step in (1, 7, 2, 6, 3, 5, 4):
        got = band_y.at[(y + NY - step) % NY]
        remote(got, got, y_s.at[step - 1], y_r.at[step - 1], sib).wait_recv()
    total = band_y[0].astype(F32)
    for j in range(1, NY):
        total = total + band_y[j].astype(F32)
    band_xz[xz] = total.astype(BF)
    for step in range(1, NXZ):
        start(remote(band_xz.at[xz], band_xz.at[xz], xz_s.at[step - 1], xz_r.at[step - 1], xz_peer(step)))
    for step in range(1, NXZ):
        got = band_xz.at[(xz + NXZ - step) % NXZ]
        remote(got, got, xz_s.at[step - 1], xz_r.at[step - 1], sib).wait_recv()
    total = band_xz[0].astype(F32)
    for j in range(1, NXZ):
        total = total + band_xz[j].astype(F32)

    def put_update(g, value):
        upd_v[g * 256 : (g + 1) * 256, :] = value.astype(BF)

    rebuild(total * (1.0 / N_DP), put_update)
    store_upd = pltpu.make_async_copy(upd_v, upd_hbm, out_sem.at[1])
    store_upd.start()
    for copy in sent:
        copy.wait_send()
    store_new.wait()
    store_upd.wait()


def on_device(tokens, key_weight, key_gain, cotangent, momentum, band_row, band_col):
    left, left_t, right = tables()
    n = len(CHUNKS)
    any_spec = pl.BlockSpec(memory_space=pl.ANY)
    smem = pl.BlockSpec(memory_space=pltpu.SMEM)
    vmem = pl.BlockSpec(memory_space=pltpu.VMEM)
    dma = pltpu.SemaphoreType.DMA
    return pl.pallas_call(
        kernel,
        out_shape=(
            jax.ShapeDtypeStruct((KV, WIDTH), BF),
            jax.ShapeDtypeStruct((1, KV, WIDTH), BF),
        ),
        in_specs=[any_spec, any_spec, vmem, any_spec, any_spec, smem, smem, any_spec, any_spec, any_spec],
        out_specs=(any_spec, any_spec),
        scratch_shapes=[
            pltpu.VMEM((NZ, 2, OWN, WIDTH), BF),
            pltpu.VMEM((KV, WIDTH), BF),
            pltpu.VMEM((NZ, 2, OWN, SPAN), BF),
            pltpu.VMEM((1, KV, WIDTH), BF),
            pltpu.VMEM(left.shape, BF),
            pltpu.VMEM(left_t.shape, BF),
            pltpu.VMEM(right.shape, BF),
            pltpu.VMEM((NZ, OWN, SPAN), BF),
            pltpu.VMEM((NZ, OWN, LANES), BF),
            pltpu.VMEM((NZ, OWN, LANES), BF),
            pltpu.VMEM((NZ, OWN, KV), BF),
            pltpu.VMEM((NZ, OWN, KV), BF),
            pltpu.VMEM((NZ, OWN, KV), BF),
            pltpu.VMEM((NZ, OWN, KV), BF),
            pltpu.VMEM((NZ - 1, OWN, KV), BF),
            pltpu.VMEM((2 * NZ, OWN, KV), BF),
            pltpu.VMEM((KV, WIDTH), F32),
            pltpu.VMEM((ROWS_BLK, BAND, WIDTH), jnp.int32),
            pltpu.VMEM((ROWS_BLK, BAND, LANES), jnp.int32),
            pltpu.VMEM((NY, 64, LANES), BF),
            pltpu.VMEM((NXZ, 64, LANES), BF),
            pltpu.VMEM((KV, WIDTH), BF),
            pltpu.VMEM((1, KV, WIDTH), BF),
            dma((6 + n,)),
            dma((2,)),
            dma(()),
            dma(()),
            dma((3,)),
            dma((3,)),
            dma((n,)),
            dma((n,)),
            dma((n, 3)),
            dma((n, 3)),
            dma((n, 3)),
            dma((n, 3)),
            dma((n, 4)),
            dma((n, 4)),
            dma((7,)),
            dma((7,)),
            dma((7,)),
            dma((7,)),
        ],
        compiler_params=pltpu.CompilerParams(
            collective_id=0, has_side_effects=True, vmem_limit_bytes=48 * 1024 * 1024
        ),
        cost_estimate=pl.CostEstimate(flops=2_500_000_000, bytes_accessed=6_000_000, transcendentals=1280),
    )(
        tokens.reshape(NZ, 2, OWN, WIDTH),
        key_weight,
        key_gain.reshape(1, KV),
        cotangent.reshape(NZ, 2, OWN, SPAN),
        momentum,
        band_row,
        band_col,
        left,
        left_t,
        right,
    )


def solution(mesh):
    return jax.shard_map(
        on_device,
        mesh=mesh,
        in_specs=(
            P("dp", "mp"),
            P(None, "mp"),
            P(),
            P("dp", "mp"),
            P("dp", None, "mp"),
            P(None, "mp"),
            P(None, "mp"),
        ),
        out_specs=(P(None, "mp"), P("dp", None, "mp")),
        check_vma=False,
    )
```

time: 472 us -> 80.5 us (0.17)
  the two profiles are of different devices: /device:TPU:128 before, /device:TPU:1 now
where the time goes in v1:
time: 80.5 us; the launch traced here: 80.1 us
  Pallas kernels  67.9 us (84%)
  local copies, waits for them, and re-layouts  11.6 us (14%)
    pallas_call x1, Pallas kernels, on_device(): pl.pallas_call(kernel, out_shape=(jax.ShapeDtypeStruct((KV, WIDTH), BF),...  67.9 us
    unnamed x21, local copies, waits for them, and re-layouts  11.6 us

profile of v1, /device:TPU:1, one launch (start us, length us, event | category | flops | bytes accessed | tf_op | source)
XLA Modules:
  0.0 80.1 jit_solution(10535090361358367266)
XLA Ops:
  0.6 1.1 %copy.12 = bf16[1280,64]{1,0:T(8,128)(2,1)S(1)} copy(bf16[1280,64]{0,1:T(8,128)(2,1)} %param.13) | data formatting | bytes 327680 | tf_op args[3]
  1.8 0.0 copy-start
  1.8 1.4 %copy-done = bf16[1280,640]{1,0:T(8,128)(2,1)S(1)} copy-done((bf16[1280,640]{1,0:T(8,128)(2,1)S(1)}, bf16[1280,640]{1,0:T(8,128)(2,1)}, u32[]{:S(2)}) %copy-start) | copy-done | bytes 1638424
  3.2 0.0 copy-start.1
  3.2 1.1 %copy-done.1 = bf16[512,640]{1,0:T(8,128)(2,1)S(1)} copy-done((bf16[512,640]{1,0:T(8,128)(2,1)S(1)}, bf16[512,640]{1,0:T(8,128)(2,1)}, u32[]{:S(2)}) %copy-start.1) | copy-done | bytes 655384
  4.3 0.0 copy-start.2
  4.3 1.1 %copy-done.2 = bf16[1,512,640]{2,1,0:T(8,128)(2,1)S(1)} copy-done((bf16[1,512,640]{2,1,0:T(8,128)(2,1)S(1)}, bf16[1,512,640]{2,1,0:T(8,128)(2,1)}, u32[]{:S(2)}) %copy-start.2) | copy-done | bytes 655384
  5.4 0.0 copy-start.3
  5.4 0.7 copy-done.3
  6.1 0.0 copy-start.4
  6.1 0.7 copy-done.4
  6.8 0.0 copy-start.5
  6.8 0.7 copy-done.5
  7.4 0.0 copy-start.6
  7.4 1.3 %copy-done.6 = bf16[2,640,512]{2,1,0:T(8,128)(2,1)S(1)} copy-done((bf16[2,640,512]{2,1,0:T(8,128)(2,1)S(1)}, bf16[2,640,512]{2,1,0:T(8,128)(2,1)}, u32[]{:S(2)}) %copy-start.6) | copy-done | bytes 1310744
  8.8 0.0 copy-start.7
  8.8 0.9 %copy-done.7 = bf16[2,256,128]{2,1,0:T(8,128)(2,1)S(1)} copy-done((bf16[2,256,128]{2,1,0:T(8,128)(2,1)S(1)}, bf16[2,256,128]{2,1,0:T(8,128)(2,1)}, u32[]{:S(2)}) %copy-start.7) | copy-done | bytes 131096
  9.7 0.0 copy-start.8
  9.7 0.9 %copy-done.8 = bf16[256,256]{1,0:T(8,128)(2,1)S(1)} copy-done((bf16[256,256]{1,0:T(8,128)(2,1)S(1)}, bf16[256,256]{1,0:T(8,128)(2,1)}, u32[]{:S(2)}) %copy-start.8) | copy-done | bytes 131096
  10.6 67.9 %shard_map.113 = (bf16[512,640]{1,0:T(8,128)(2,1)S(1)}, bf16[1,512,640]{2,1,0:T(8,128)(2,1)S(1)}) custom-call(bf16[4,2,160,640]{3,2,1,0:T(8,128)(2,1)S(1)} %bitcast.4, bf16[512,640]{1,0:T(8,128)(2,1)S(1)} %copy-done.1, f32[1,512]{1,0:T(1,128)S(1)} %bitcast.5, bf16[4,2,160,64]{3,2,1,0:T(8,128)(2,1)S(1)} %bitcast.3, bf16[1,512,640]{2,1,0:T(8,128)(2,1)S(1)} %copy-done.2, ...), custom_call_target="tpu_custom_call" | custom-call | flops 2500000000 | bytes 6000000 | tf_op jit(solution)/shard_map/pallas_call | solution.py:300
  78.4 0.8 %copy.15 = bf16[512,640]{1,0:T(8,128)(2,1)} copy(bf16[512,640]{1,0:T(8,128)(2,1)S(1)} %get-tuple-element.4) | data formatting | bytes 1310720
  79.3 0.8 %copy.16 = bf16[1,512,640]{2,1,0:T(8,128)(2,1)} copy(bf16[1,512,640]{2,1,0:T(8,128)(2,1)S(1)} %get-tuple-element.5) | data formatting | bytes 1310720
Async XLA Ops:
  1.8 1.4 %copy-start = (bf16[1280,640]{1,0:T(8,128)(2,1)S(1)}, bf16[1280,640]{1,0:T(8,128)(2,1)}, u32[]{:S(2)}) copy-start(bf16[1280,640]{1,0:T(8,128)(2,1)} %param.10) | copy-start | bytes 4915204
  3.2 1.1 %copy-start.1 = (bf16[512,640]{1,0:T(8,128)(2,1)S(1)}, bf16[512,640]{1,0:T(8,128)(2,1)}, u32[]{:S(2)}) copy-start(bf16[512,640]{1,0:T(8,128)(2,1)} %w_hbm.1) | copy-start | bytes 1966084
  4.3 1.1 %copy-start.2 = (bf16[1,512,640]{2,1,0:T(8,128)(2,1)S(1)}, bf16[1,512,640]{2,1,0:T(8,128)(2,1)}, u32[]{:S(2)}) copy-start(bf16[1,512,640]{2,1,0:T(8,128)(2,1)} %mom_hbm.1) | copy-start | bytes 1966084
  5.4 0.7 copy-start.3
  6.1 0.7 copy-start.4
  6.8 0.7 copy-start.5
  7.4 1.3 %copy-start.6 = (bf16[2,640,512]{2,1,0:T(8,128)(2,1)S(1)}, bf16[2,640,512]{2,1,0:T(8,128)(2,1)}, u32[]{:S(2)}) copy-start(bf16[2,640,512]{2,1,0:T(8,128)(2,1)} %constant.8.clone.right_hbm) | copy-start | bytes 3932164
  8.8 0.9 %copy-start.7 = (bf16[2,256,128]{2,1,0:T(8,128)(2,1)S(1)}, bf16[2,256,128]{2,1,0:T(8,128)(2,1)}, u32[]{:S(2)}) copy-start(bf16[2,256,128]{2,1,0:T(8,128)(2,1)} %constant.7.clone.left_t_hbm) | copy-start | bytes 393220
  9.7 0.9 %copy-start.8 = (bf16[256,256]{1,0:T(8,128)(2,1)S(1)}, bf16[256,256]{1,0:T(8,128)(2,1)}, u32[]{:S(2)}) copy-start(bf16[256,256]{1,0:T(8,128)(2,1)} %constant.6.clone.left_hbm) | copy-start | bytes 393220

commit v2 on v1

--- a/solution.py
+++ b/solution.py
@@ -31,12 +31,13 @@
 COLS_BLK = WIDTH // SPAN
 LANES = 128
 CHUNKS = ((0, 80), (80, 80))
+WAYS = ((1, slice(0, 256)), (3, slice(256, 512)))
 
 
 def split_const(table):
     high = table.astype(np.float32).astype(ml_dtypes.bfloat16)
     low = (table - high.astype(np.float64)).astype(np.float32).astype(ml_dtypes.bfloat16)
-    return high, low
+    return high.astype(np.float32), low.astype(np.float32)
 
 
 def tables():
@@ -45,18 +46,13 @@
     c = np.cos(np.pi * (2.0 * n + 1.0) * f / (2.0 * SPAN))
     c = c * np.where(f == 0, np.sqrt(1.0 / SPAN), np.sqrt(2.0 / SPAN))
     c = c[:LOW]
-    left = np.kron(np.eye(4), c)
-    right = np.zeros((COLS_BLK, SPAN, OFFSETS, LANES))
-    for block in range(COLS_BLK):
-        for band in range(OFFSETS):
-            right[block, :, band, block * BAND : (block + 1) * BAND] = c[band * BAND : (band + 1) * BAND].T
-    right = right.reshape(WIDTH, OFFSETS * LANES)
-    lh, ll = split_const(left)
-    rh, rl = split_const(right)
+    high, low = split_const(np.kron(np.eye(4), c))
+    right = np.zeros((SPAN, OFFSETS, LANES // BAND, BAND))
+    right[:] = c.T.reshape(SPAN, OFFSETS, 1, BAND)
     return (
-        np.concatenate([lh, ll], axis=0),
-        np.stack([np.ascontiguousarray(lh.T), np.ascontiguousarray(ll.T)]),
-        np.stack([rh, rl]),
+        np.concatenate([high, low], axis=0),
+        np.stack([np.ascontiguousarray(high.T), np.ascontiguousarray(low.T)]),
+        np.stack(split_const(right.reshape(SPAN, OFFSETS * LANES))),
     )
 
 
@@ -72,10 +68,10 @@
 def kernel(
     x_hbm, w_hbm, gain_ref, cot_hbm, mom_hbm, row_ref, col_ref, left_hbm, left_t_hbm, right_hbm,
     upd_hbm, new_hbm,
-    xv, wv, cotv, momv, leftv, left_tv, rightv,
-    cot_sib, cot_mix, cot_all, part_out, part_own, part_in, pair, recv, dk, mom_new,
+    xv, wv, momv, left_f, left_t_f, right_f, leftv, left_tv, rightv,
+    cot_pair, cot_mix, cot_all, part_out, part_own, part_in, pair, relay, relay_sum, recv, dk, mom_new,
     row_mask, col_mask, band_y, band_xz, upd_v, new_v,
-    load_sem, out_sem, cs_s, cs_r, cz_s, cz_r, ps_s, ps_r, rs_s, rs_r, ag_s, ag_r, fw_s, fw_r,
+    load_sem, out_sem, cs_s, cs_r, cz_s, cz_r, ps_s, ps_r, r1_s, r1_r, rd_s, rd_r, r2_s, r2_r, ag_s, ag_r, a2_s, a2_r, fw_s, fw_r,
     y_s, y_r, xz_s, xz_r,
 ):
     dp = lax.axis_index("dp")
@@ -106,7 +102,8 @@
         at = (slice(None), slice(None), pl.ds(off, rows))
         loads.append(pltpu.make_async_copy(x_hbm.at[at], xv.at[at], load_sem.at[1 + k]))
     base = 1 + len(CHUNKS)
-    more = [(cot_hbm, cotv), (mom_hbm, momv), (left_hbm, leftv), (left_t_hbm, left_tv), (right_hbm, rightv)]
+    more = [(cot_hbm, cot_pair.at[core]), (mom_hbm, momv)]
+    more += [(left_hbm, left_f), (left_t_hbm, left_t_f), (right_hbm, right_f)]
     for k, (src, dst) in enumerate(more):
         loads.append(pltpu.make_async_copy(src, dst, load_sem.at[base + k]))
     for load in loads:
@@ -118,13 +115,21 @@
         )
 
     sent = []
-
-    def start(copy):
+    flying = {}
+
+    def start(key, copy):
         copy.start()
         sent.append(copy)
-
-    loads[0].wait()
-    for k, (off, rows) in enumerate(CHUNKS):
+        flying[key] = copy
+
+    def landed(key, copy):
+        copy.wait_recv()
+        del flying[key]
+
+    part_swaps = []
+
+    def partial_keys(k):
+        off, rows = CHUNKS[k]
         loads[1 + k].wait()
         at = pl.ds(off, rows)
         for side, place in ((1 - core, part_out), (core, part_own)):
@@ -132,38 +137,56 @@
             part = dot(x_rows, wv[...], ((1,), (1,)))
             place[:, at, :] = part.astype(BF).reshape(NZ, rows, KV)
 
+    def swap_parts(k):
+        at = (slice(None), pl.ds(*CHUNKS[k]))
+        part_swaps.append(remote(part_out.at[at], part_in.at[at], ps_s.at[k], ps_r.at[k], sib))
+        start(("ps", k), part_swaps[k])
+
+    loads[0].wait()
+    partial_keys(0)
+    pl.semaphore_wait(barrier, len(peers))
+    swap_parts(0)
+    cot_swap = remote(cot_hbm, cot_pair.at[core], cs_s, cs_r, sib)
+    start(("cs",), cot_swap)
+    for k in range(1, len(CHUNKS)):
+        partial_keys(k)
+        swap_parts(k)
+
+    for k, (off, rows) in enumerate(CHUNKS):
+        at = pl.ds(off, rows)
+        landed(("ps", k), part_swaps[k])
+        pair[:, at, :] = (part_own[:, at, :].astype(F32) + part_in[:, at, :].astype(F32)).astype(BF)
+        for way, (step, half) in enumerate(WAYS):
+            start(("r1", k, way), remote(
+                pair.at[(zh + 2) % NZ, at, half], relay.at[way, at], r1_s.at[k, way], r1_r.at[k, way], z_peer(step)
+            ))
+
     loads[base].wait()
-    pl.semaphore_wait(barrier, len(peers))
-
-    cot_swap = remote(cotv.at[:, 1 - core], cot_sib, cs_s, cs_r, sib)
-    start(cot_swap)
-    part_swaps = []
-    for k, (off, rows) in enumerate(CHUNKS):
-        at = (slice(None), pl.ds(off, rows))
-        part_swaps.append(remote(part_out.at[at], part_in.at[at], ps_s.at[k], ps_r.at[k], sib))
-        start(part_swaps[-1])
-
-    cot_swap.wait_recv()
-    feature = lax.broadcasted_iota(jnp.int32, (SPAN, LANES), 0)
-    lane = lax.broadcasted_iota(jnp.int32, (SPAN, LANES), 1)
-    put_own = (lane == feature + core * SPAN).astype(BF)
-    put_sib = (lane == feature + (1 - core) * SPAN).astype(BF)
-    mixed = dot(cotv[:, core].reshape(NZ * OWN, SPAN), put_own) + dot(cot_sib[...].reshape(NZ * OWN, SPAN), put_sib)
-    cot_mix[...] = mixed.astype(BF).reshape(NZ, OWN, LANES)
-    cot_all[zh] = cot_mix[zh]
+    landed(("cs",), cot_swap)
+    cot_mix[...] = cot_pair[...].reshape(LANES, 2 * NZ * OWN).T.reshape(NZ, 2, OWN, LANES)
+    cot_all[zh] = cot_mix[zh, core]
     for step in (2, 1, 3):
-        start(remote(
-            cot_mix.at[(zh + step) % NZ], cot_all.at[zh], cz_s.at[step - 1], cz_r.at[step - 1], z_peer(step)
+        start(("cz", step), remote(
+            cot_mix.at[(zh + step) % NZ, core], cot_all.at[zh], cz_s.at[step - 1], cz_r.at[step - 1], z_peer(step)
         ))
-
-    for k, (off, rows) in enumerate(CHUNKS):
-        at = pl.ds(off, rows)
-        part_swaps[k].wait_recv()
-        pair[:, at, :] = (part_own[:, at, :].astype(F32) + part_in[:, at, :].astype(F32)).astype(BF)
-        for step in (2, 1, 3):
-            start(remote(
-                pair.at[(zh + step) % NZ, at], recv.at[step - 1, at],
-                rs_s.at[k, step - 1], rs_r.at[k, step - 1], z_peer(step),
+    for k, (off, rows) in enumerate(CHUNKS):
+        at = pl.ds(off, rows)
+        for way, (step, half) in enumerate(WAYS):
+            other = WAYS[1 - way][1]
+            start(("rd", k, way), remote(
+                pair.at[(zh + step) % NZ, at, other], recv.at[way, at, other],
+                rd_s.at[k, way], rd_r.at[k, way], z_peer(step),
+            ))
+    for k, (off, rows) in enumerate(CHUNKS):
+        at = pl.ds(off, rows)
+        for way, (step, half) in enumerate(WAYS):
+            landed(("r1", k, way), remote(
+                pair.at[0, at, half], relay.at[way, at], r1_s.at[k, way], r1_r.at[k, way], sib
+            ))
+            both = pair[(zh + step) % NZ, at, half].astype(F32) + relay[way, at, :].astype(F32)
+            relay_sum[way, at, :] = both.astype(BF)
+            start(("r2", k, way), remote(
+                relay_sum.at[way, at], recv.at[way, at, half], r2_s.at[k, way], r2_r.at[k, way], z_peer(step)
             ))
 
     block_r = lax.broadcasted_iota(jnp.int32, (BAND, WIDTH), 1) // SPAN
@@ -183,35 +206,59 @@
     for load in loads[base + 1 :]:
         load.wait()
     mom_new[...] = DECAY * momv[0].astype(F32)
+    leftv[...] = left_f[...].astype(BF)
+    left_tv[...] = left_t_f[...].astype(BF)
+    lane_block = (lax.broadcasted_iota(jnp.int32, (SPAN, OFFSETS * LANES), 1) % LANES) // BAND
+    for c in range(COLS_BLK):
+        for part in range(2):
+            rightv[part, c * SPAN : (c + 1) * SPAN] = jnp.where(lane_block == c, right_f[part], 0.0).astype(BF)
 
     for step in (2, 1, 3):
         src = (zh + NZ - step) % NZ
-        remote(cot_mix.at[0], cot_all.at[src], cz_s.at[step - 1], cz_r.at[step - 1], sib).wait_recv()
+        landed(("cz", step), remote(cot_mix.at[0, 0], cot_all.at[src], cz_s.at[step - 1], cz_r.at[step - 1], sib))
     gain = gain_ref[...]
     for k, (off, rows) in enumerate(CHUNKS):
         at = pl.ds(off, rows)
-        keys = pair[zh, at, :].astype(F32)
-        for step in (1, 3, 2):
-            remote(pair.at[0, at], recv.at[step - 1, at], rs_s.at[k, step - 1], rs_r.at[k, step - 1], sib).wait_recv()
-            keys = keys + recv[step - 1, at, :].astype(F32)
+        for way, (step, half) in enumerate(WAYS):
+            other = WAYS[1 - way][1]
+            landed(("rd", k, way), remote(
+                pair.at[0, at, other], recv.at[way, at, other], rd_s.at[k, way], rd_r.at[k, way], sib
+            ))
+        for way, (step, half) in enumerate(WAYS):
+            landed(("r2", k, way), remote(
+                relay_sum.at[way, at], recv.at[way, at, half], r2_s.at[k, way], r2_r.at[k, way], sib
+            ))
+        keys = pair[zh, at, :].astype(F32) + recv[0, at, :].astype(F32) + recv[1, at, :].astype(F32)
         scaled = gain * jnp.concatenate([cot_all[j, at, :].astype(F32) for j in range(NZ)], axis=-1)
         inverse = lax.rsqrt(jnp.mean(keys * keys, axis=-1, keepdims=True) + EPS)
         inner = jnp.sum(scaled * keys, axis=-1, keepdims=True)
         dk[mp, at, :] = (inverse * scaled - (inverse * inverse * inverse * inner / KV) * keys).astype(BF)
-        for step in (2, 1, 3):
-            start(remote(dk.at[mp, at], dk.at[mp, at], ag_s.at[k, step - 1], ag_r.at[k, step - 1], z_peer(step)))
-        start(remote(dk.at[mp, at], dk.at[mp, at], fw_s.at[k, 0], fw_r.at[k, 0], sib))
-
-    for k, (off, rows) in enumerate(CHUNKS):
-        at = pl.ds(off, rows)
-        for step in (1, 3, 2):
-            src = ((zh + NZ - step) % NZ) * 2 + core
-            got = dk.at[src, at]
-            remote(got, got, ag_s.at[k, step - 1], ag_r.at[k, step - 1], sib).wait_recv()
-            start(remote(got, got, fw_s.at[k, step], fw_r.at[k, step], sib))
+        mine = dk.at[mp, at]
+        for way, (step, half) in enumerate(WAYS):
+            start(("ag", k, way), remote(mine, mine, ag_s.at[k, way], ag_r.at[k, way], z_peer(step)))
+        start(("fw", k, 0), remote(mine, mine, fw_s.at[k, 0], fw_r.at[k, 0], sib))
+
+    def owner(step, side):
+        return ((zh + NZ - step) % NZ) * 2 + side
+
+    for k, (off, rows) in enumerate(CHUNKS):
+        at = pl.ds(off, rows)
+        for way, (step, half) in enumerate(WAYS):
+            got = dk.at[owner(step, core), at]
+            landed(("ag", k, way), remote(got, got, ag_s.at[k, way], ag_r.at[k, way], sib))
+            part = dk.at[owner(step, core), at, half]
+            start(("a2", k, way), remote(part, part, a2_s.at[k, way], a2_r.at[k, way], z_peer(step)))
+            start(("fw", k, step), remote(got, got, fw_s.at[k, step], fw_r.at[k, step], sib))
+    for k, (off, rows) in enumerate(CHUNKS):
+        at = pl.ds(off, rows)
+        for way, (step, half) in enumerate(WAYS):
+            part = dk.at[owner(2, core), at, half]
+            landed(("a2", k, way), remote(part, part, a2_s.at[k, way], a2_r.at[k, way], sib))
+        got = dk.at[owner(2, core), at]
+        start(("fw", k, 2), remote(got, got, fw_s.at[k, 2], fw_r.at[k, 2], sib))
         for step in (0, 1, 3, 2):
-            got = dk.at[((zh + NZ - step) % NZ) * 2 + 1 - core, at]
-            remote(got, got, fw_s.at[k, step], fw_r.at[k, step], sib).wait_recv()
+            got = dk.at[owner(step, 1 - core), at]
+            landed(("fw", k, step), remote(got, got, fw_s.at[k, step], fw_r.at[k, step], sib))
         all_dk = dk[:, at, :].reshape(2 * NZ * rows, KV)
         all_x = xv[:, :, at, :].reshape(2 * NZ * rows, WIDTH)
         mom_new[...] += dot(all_dk, all_x, ((0,), (0,))) * (1.0 / math.sqrt(2 * NZ * OWN))
@@ -238,7 +285,7 @@
 
     band_y[y] = coeffs.astype(BF)
     for step in (4, 3, 5, 2, 6, 1, 7):
-        start(remote(band_y.at[y], band_y.at[y], y_s.at[step - 1], y_r.at[step - 1], y_peer(step)))
+        start(("y", step), remote(band_y.at[y], band_y.at[y], y_s.at[step - 1], y_r.at[step - 1], y_peer(step)))
 
     def rebuild(values, put):
         parts = [jnp.where(chosen == band, values, 0.0) for band in range(OFFSETS)]
@@ -264,16 +311,16 @@
 
     for step in (1, 7, 2, 6, 3, 5, 4):
         got = band_y.at[(y + NY - step) % NY]
-        remote(got, got, y_s.at[step - 1], y_r.at[step - 1], sib).wait_recv()
+        landed(("y", step), remote(got, got, y_s.at[step - 1], y_r.at[step - 1], sib))
     total = band_y[0].astype(F32)
     for j in range(1, NY):
         total = total + band_y[j].astype(F32)
     band_xz[xz] = total.astype(BF)
     for step in range(1, NXZ):
-        start(remote(band_xz.at[xz], band_xz.at[xz], xz_s.at[step - 1], xz_r.at[step - 1], xz_peer(step)))
+        start(("xz", step), remote(band_xz.at[xz], band_xz.at[xz], xz_s.at[step - 1], xz_r.at[step - 1], xz_peer(step)))
     for step in range(1, NXZ):
         got = band_xz.at[(xz + NXZ - step) % NXZ]
-        remote(got, got, xz_s.at[step - 1], xz_r.at[step - 1], sib).wait_recv()
+        landed(("xz", step), remote(got, got, xz_s.at[step - 1], xz_r.at[step - 1], sib))
     total = band_xz[0].astype(F32)
     for j in range(1, NXZ):
         total = total + band_xz[j].astype(F32)
@@ -293,7 +340,7 @@
 def on_device(tokens, key_weight, key_gain, cotangent, momentum, band_row, band_col):
     left, left_t, right = tables()
     n = len(CHUNKS)
-    any_spec = pl.BlockSpec(memory_space=pl.ANY)
+    any_spec = pl.BlockSpec(memory_space=pltpu.HBM)
     smem = pl.BlockSpec(memory_space=pltpu.SMEM)
     vmem = pl.BlockSpec(memory_space=pltpu.VMEM)
     dma = pltpu.SemaphoreType.DMA
@@ -308,19 +355,23 @@
         scratch_shapes=[
             pltpu.VMEM((NZ, 2, OWN, WIDTH), BF),
             pltpu.VMEM((KV, WIDTH), BF),
-            pltpu.VMEM((NZ, 2, OWN, SPAN), BF),
             pltpu.VMEM((1, KV, WIDTH), BF),
+            pltpu.VMEM(left.shape, F32),
+            pltpu.VMEM(left_t.shape, F32),
+            pltpu.VMEM(right.shape, F32),
             pltpu.VMEM(left.shape, BF),
             pltpu.VMEM(left_t.shape, BF),
-            pltpu.VMEM(right.shape, BF),
-            pltpu.VMEM((NZ, OWN, SPAN), BF),
-            pltpu.VMEM((NZ, OWN, LANES), BF),
+            pltpu.VMEM((2, WIDTH, OFFSETS * LANES), BF),
+            pltpu.VMEM((2, SPAN, 2 * NZ * OWN), BF),
+            pltpu.VMEM((NZ, 2, OWN, LANES), BF),
             pltpu.VMEM((NZ, OWN, LANES), BF),
             pltpu.VMEM((NZ, OWN, KV), BF),
             pltpu.VMEM((NZ, OWN, KV), BF),
             pltpu.VMEM((NZ, OWN, KV), BF),
             pltpu.VMEM((NZ, OWN, KV), BF),
-            pltpu.VMEM((NZ - 1, OWN, KV), BF),
+            pltpu.VMEM((2, OWN, KV // 2), BF),
+            pltpu.VMEM((2, OWN, KV // 2), BF),
+            pltpu.VMEM((2, OWN, KV), BF),
             pltpu.VMEM((2 * NZ, OWN, KV), BF),
             pltpu.VMEM((KV, WIDTH), F32),
             pltpu.VMEM((ROWS_BLK, BAND, WIDTH), jnp.int32),
@@ -337,10 +388,16 @@
             dma((3,)),
             dma((n,)),
             dma((n,)),
-            dma((n, 3)),
-            dma((n, 3)),
-            dma((n, 3)),
-            dma((n, 3)),
+            dma((n, 2)),
+            dma((n, 2)),
+            dma((n, 2)),
+            dma((n, 2)),
+            dma((n, 2)),
+            dma((n, 2)),
+            dma((n, 2)),
+            dma((n, 2)),
+            dma((n, 2)),
+            dma((n, 2)),
             dma((n, 4)),
             dma((n, 4)),
             dma((7,)),
@@ -349,14 +406,14 @@
             dma((7,)),
         ],
         compiler_params=pltpu.CompilerParams(
-            collective_id=0, has_side_effects=True, vmem_limit_bytes=48 * 1024 * 1024
+            collective_id=0, has_side_effects=True, vmem_limit_bytes=64 * 1024 * 1024
         ),
         cost_estimate=pl.CostEstimate(flops=2_500_000_000, bytes_accessed=6_000_000, transcendentals=1280),
     )(
         tokens.reshape(NZ, 2, OWN, WIDTH),
         key_weight,
         key_gain.reshape(1, KV),
-        cotangent.reshape(NZ, 2, OWN, SPAN),
+        cotangent.T,
         momentum,
         band_row,
         band_col,

time: 80.5 us -> 67.2 us (0.83)
  local copies, waits for them, and re-layouts: 11.6 us -> 2.89 us
  Pallas kernels: 67.9 us -> 63.4 us
    unnamed x21 -> x4, local copies, waits for them, and re-layouts: 11.6 us -> 2.89 us
    pallas_call x1, Pallas kernels: 67.9 us -> 63.4 us  [on_device(): pl.pallas_call(kernel, out_shape=(jax.ShapeDtypeStruct((KV, WIDTH), BF),...]
where the time goes in v2:
time: 67.2 us; the launch traced here: 67 us
  Pallas kernels  63.4 us (94%)
  local copies, waits for them, and re-layouts  2.89 us (4%)
    pallas_call x1, Pallas kernels, on_device(): pl.pallas_call(kernel, out_shape=(jax.ShapeDtypeStruct((KV, WIDTH), BF),...  63.4 us
    unnamed x4, local copies, waits for them, and re-layouts  2.89 us

profile of v2, /device:TPU:1, one launch (start us, length us, event | category | flops | bytes accessed | tf_op | source)
XLA Modules:
  0.0 67.0 jit_solution(3353587601692987419)
XLA Ops:
  0.6 63.4 %shard_map.113 = (bf16[512,640]{1,0:T(8,128)(2,1)}, bf16[1,512,640]{2,1,0:T(8,128)(2,1)}) custom-call(bf16[4,2,160,640]{3,2,1,0:T(8,128)(2,1)} %bitcast.3, bf16[512,640]{1,0:T(8,128)(2,1)} %w_hbm.1, f32[1,512]{1,0:T(1,128)} %bitcast.5, bf16[64,1280]{1,0:T(8,128)(2,1)} %bitcast.4, bf16[1,512,640]{2,1,0:T(8,128)(2,1)} %mom_hbm.1, s32[8,10]{1,0:T(8,128)} %row_ref.1, ...), custom_call_target="tpu_custom_call" | custom-call | flops 2500000000 | bytes 6000000 | tf_op jit(solution)/shard_map/pallas_call | solution.py:347
  64.1 0.0 copy-start
  64.1 2.0 %copy.14 = bf16[512,640]{1,0:T(8,128)(2,1)} copy(bf16[512,640]{1,0:T(8,128)(2,1)} %get-tuple-element.4) | data formatting | bytes 1310720
  66.1 0.0 copy-done
  66.1 0.8 %copy.15 = bf16[1,512,640]{2,1,0:T(8,128)(2,1)} copy(bf16[1,512,640]{2,1,0:T(8,128)(2,1)S(1)} %copy-done) | data formatting | bytes 1310720
Async XLA Ops:
  64.1 2.1 %copy-start = (bf16[1,512,640]{2,1,0:T(8,128)(2,1)S(1)}, bf16[1,512,640]{2,1,0:T(8,128)(2,1)}, u32[]{:S(2)}) copy-start(bf16[1,512,640]{2,1,0:T(8,128)(2,1)} %get-tuple-element.5) | copy-start | bytes 1966084

commit v3 on v2

--- a/solution.py
+++ b/solution.py
@@ -66,12 +66,12 @@
 
 
 def kernel(
-    x_hbm, w_hbm, gain_ref, cot_hbm, mom_hbm, row_ref, col_ref, left_hbm, left_t_hbm, right_hbm,
-    upd_hbm, new_hbm,
-    xv, wv, momv, left_f, left_t_f, right_f, leftv, left_tv, rightv,
+    x_hbm, w_hbm, gain_hbm, cot_hbm, mom_hbm, row_hbm, col_hbm, left_hbm, left_t_hbm, right_hbm,
+    upd_v, new_v,
+    xv, wv, gain_ref, row_ref, col_ref, momv, left_f, left_t_f, right_f, leftv, left_tv, rightv,
     cot_pair, cot_mix, cot_all, part_out, part_own, part_in, pair, relay, relay_sum, recv, dk, mom_new,
-    row_mask, col_mask, band_y, band_xz, upd_v, new_v,
-    load_sem, out_sem, cs_s, cs_r, cz_s, cz_r, ps_s, ps_r, r1_s, r1_r, rd_s, rd_r, r2_s, r2_r, ag_s, ag_r, a2_s, a2_r, fw_s, fw_r,
+    row_mask, col_mask, band_y, band_xz,
+    load_sem, cs_s, cs_r, cz_s, cz_r, ps_s, ps_r, r1_s, r1_r, rd_s, rd_r, r2_s, r2_r, ag_s, ag_r, a2_s, a2_r, fw_s, fw_r,
     y_s, y_r, xz_s, xz_r,
 ):
     dp = lax.axis_index("dp")
@@ -92,21 +92,27 @@
         return {"dp": ((xz + step) % NXZ) * NY + y, "mp": mp}
 
     barrier = pltpu.get_barrier_semaphore()
-    peers = [y_peer(s) for s in (4, 3, 5, 2, 6, 1, 7)] + [xz_peer(s) for s in range(1, NXZ)]
-    peers += [z_peer(s) for s in (2, 1, 3)] + [sib]
-    for peer in peers:
-        pl.semaphore_signal(barrier, inc=1, device_id=peer, device_id_type=MESH)
-
+    near = [z_peer(s) for s in (2, 1, 3)] + [sib]
+    far = [y_peer(s) for s in (4, 3, 5, 2, 6, 1, 7)] + [xz_peer(s) for s in range(1, NXZ)]
+
+    def greet(peers):
+        for peer in peers:
+            pl.semaphore_signal(barrier, inc=1, device_id=peer, device_id_type=MESH)
+
+    greet(near)
     loads = [pltpu.make_async_copy(w_hbm, wv, load_sem.at[0])]
     for k, (off, rows) in enumerate(CHUNKS):
         at = (slice(None), slice(None), pl.ds(off, rows))
         loads.append(pltpu.make_async_copy(x_hbm.at[at], xv.at[at], load_sem.at[1 + k]))
     base = 1 + len(CHUNKS)
-    more = [(cot_hbm, cot_pair.at[core]), (mom_hbm, momv)]
+    more = [(cot_hbm, cot_pair.at[core]), (gain_hbm, gain_ref), (row_hbm, row_ref), (col_hbm, col_ref), (mom_hbm, momv)]
     more += [(left_hbm, left_f), (left_t_hbm, left_t_f), (right_hbm, right_f)]
     for k, (src, dst) in enumerate(more):
         loads.append(pltpu.make_async_copy(src, dst, load_sem.at[base + k]))
-    for load in loads:
+    for load in loads[: base + 1]:
+        load.start()
+    greet(far)
+    for load in loads[base + 1 :]:
         load.start()
 
     def remote(src, dst, send, recv_, peer):
@@ -143,14 +149,13 @@
         start(("ps", k), part_swaps[k])
 
     loads[0].wait()
-    partial_keys(0)
-    pl.semaphore_wait(barrier, len(peers))
-    swap_parts(0)
+    for k in range(len(CHUNKS)):
+        partial_keys(k)
+    pl.semaphore_wait(barrier, len(near) + len(far))
+    for k in range(len(CHUNKS)):
+        swap_parts(k)
     cot_swap = remote(cot_hbm, cot_pair.at[core], cs_s, cs_r, sib)
     start(("cs",), cot_swap)
-    for k in range(1, len(CHUNKS)):
-        partial_keys(k)
-        swap_parts(k)
 
     for k, (off, rows) in enumerate(CHUNKS):
         at = pl.ds(off, rows)
@@ -202,9 +207,9 @@
         col_mask[r] = of_col
         return carry
 
-    lax.fori_loop(0, ROWS_BLK, spread, 0)
     for load in loads[base + 1 :]:
         load.wait()
+    lax.fori_loop(0, ROWS_BLK, spread, 0)
     mom_new[...] = DECAY * momv[0].astype(F32)
     leftv[...] = left_f[...].astype(BF)
     left_tv[...] = left_t_f[...].astype(BF)
@@ -287,27 +292,30 @@
     for step in (4, 3, 5, 2, 6, 1, 7):
         start(("y", step), remote(band_y.at[y], band_y.at[y], y_s.at[step - 1], y_r.at[step - 1], y_peer(step)))
 
-    def rebuild(values, put):
+    def rebuild(values, exact, put):
         parts = [jnp.where(chosen == band, values, 0.0) for band in range(OFFSETS)]
         high, low = split(jnp.concatenate(parts, axis=1))
-        both = dot(jnp.concatenate([high, low], axis=0), rightv[0], ((1,), (1,)))
-        first = both[:64] + both[64:] + dot(high, rightv[1], ((1,), (1,)))
+        if exact:
+            both = dot(jnp.concatenate([high, low], axis=0), rightv[0], ((1,), (1,)))
+            first = both[:64] + both[64:] + dot(high, rightv[1], ((1,), (1,)))
+        else:
+            first = dot(high, rightv[0], ((1,), (1,)))
         for g in range(2):
             rows = first[g * 32 : (g + 1) * 32].reshape(4, 1, BAND, WIDTH)
             bands = lax.broadcasted_iota(jnp.int32, (4, OFFSETS, BAND, WIDTH), 1)
             mask = row_mask[g * 4 : (g + 1) * 4].reshape(4, 1, BAND, WIDTH)
             spread_rows = jnp.where(mask == bands, rows, 0.0).reshape(128, WIDTH)
             high, low = split(spread_rows)
-            out = dot(left_tv[0], high) + dot(left_tv[1], high) + dot(left_tv[0], low)
+            out = dot(left_tv[0], high)
+            if exact:
+                out = out + dot(left_tv[1], high) + dot(left_tv[0], low)
             put(g, out)
 
     def put_new(g, own):
         at = slice(g * 256, (g + 1) * 256)
         new_v[0, at, :] = (mom_new[at, :] - own).astype(BF)
 
-    rebuild(coeffs, put_new)
-    store_new = pltpu.make_async_copy(new_v, new_hbm, out_sem.at[0])
-    store_new.start()
+    rebuild(coeffs, True, put_new)
 
     for step in (1, 7, 2, 6, 3, 5, 4):
         got = band_y.at[(y + NY - step) % NY]
@@ -328,20 +336,19 @@
     def put_update(g, value):
         upd_v[g * 256 : (g + 1) * 256, :] = value.astype(BF)
 
-    rebuild(total * (1.0 / N_DP), put_update)
-    store_upd = pltpu.make_async_copy(upd_v, upd_hbm, out_sem.at[1])
-    store_upd.start()
+    rebuild(total * (1.0 / N_DP), False, put_update)
     for copy in sent:
         copy.wait_send()
-    store_new.wait()
-    store_upd.wait()
+
+
+def hbm(value):
+    return pltpu.with_memory_space_constraint(value, pltpu.HBM)
 
 
 def on_device(tokens, key_weight, key_gain, cotangent, momentum, band_row, band_col):
     left, left_t, right = tables()
     n = len(CHUNKS)
     any_spec = pl.BlockSpec(memory_space=pltpu.HBM)
-    smem = pl.BlockSpec(memory_space=pltpu.SMEM)
     vmem = pl.BlockSpec(memory_space=pltpu.VMEM)
     dma = pltpu.SemaphoreType.DMA
     return pl.pallas_call(
@@ -350,11 +357,14 @@
             jax.ShapeDtypeStruct((KV, WIDTH), BF),
             jax.ShapeDtypeStruct((1, KV, WIDTH), BF),
         ),
-        in_specs=[any_spec, any_spec, vmem, any_spec, any_spec, smem, smem, any_spec, any_spec, any_spec],
-        out_specs=(any_spec, any_spec),
+        in_specs=[any_spec] * 10,
+        out_specs=(vmem, vmem),
         scratch_shapes=[
             pltpu.VMEM((NZ, 2, OWN, WIDTH), BF),
             pltpu.VMEM((KV, WIDTH), BF),
+            pltpu.VMEM((1, KV), F32),
+            pltpu.SMEM((ROWS_BLK, COLS_BLK), jnp.int32),
+            pltpu.SMEM((ROWS_BLK, COLS_BLK), jnp.int32),
             pltpu.VMEM((1, KV, WIDTH), BF),
             pltpu.VMEM(left.shape, F32),
             pltpu.VMEM(left_t.shape, F32),
@@ -378,10 +388,7 @@
             pltpu.VMEM((ROWS_BLK, BAND, LANES), jnp.int32),
             pltpu.VMEM((NY, 64, LANES), BF),
             pltpu.VMEM((NXZ, 64, LANES), BF),
-            pltpu.VMEM((KV, WIDTH), BF),
-            pltpu.VMEM((1, KV, WIDTH), BF),
-            dma((6 + n,)),
-            dma((2,)),
+            dma((9 + n,)),
             dma(()),
             dma(()),
             dma((3,)),
@@ -406,20 +413,20 @@
             dma((7,)),
         ],
         compiler_params=pltpu.CompilerParams(
-            collective_id=0, has_side_effects=True, vmem_limit_bytes=64 * 1024 * 1024
+            collective_id=0, has_side_effects=True, vmem_limit_bytes=48 * 1024 * 1024
         ),
         cost_estimate=pl.CostEstimate(flops=2_500_000_000, bytes_accessed=6_000_000, transcendentals=1280),
     )(
-        tokens.reshape(NZ, 2, OWN, WIDTH),
-        key_weight,
-        key_gain.reshape(1, KV),
-        cotangent.T,
-        momentum,
-        band_row,
-        band_col,
-        left,
-        left_t,
-        right,
+        hbm(tokens.reshape(NZ, 2, OWN, WIDTH)),
+        hbm(key_weight),
+        hbm(key_gain.reshape(1, KV)),
+        hbm(cotangent.T),
+        hbm(momentum),
+        hbm(band_row),
+        hbm(band_col),
+        hbm(left),
+        hbm(left_t),
+        hbm(right),
     )
 
 

time: 67.2 us -> 63.5 us (0.945)
  Pallas kernels: 63.4 us -> 61 us
  local copies, waits for them, and re-layouts: 2.89 us -> 1.67 us
    pallas_call x1, Pallas kernels: 63.4 us -> 61 us  [on_device(): pl.pallas_call(kernel, out_shape=(jax.ShapeDtypeStruct((KV, WIDTH), BF),...]
    unnamed x4 -> x2, local copies, waits for them, and re-layouts: 2.89 us -> 1.67 us
where the time goes in v3:
time: 63.5 us; the launch traced here: 63.3 us
  Pallas kernels  61 us (96%)
  local copies, waits for them, and re-layouts  1.67 us (3%)
  between operations  0.64 us (1%)
    pallas_call x1, Pallas kernels, on_device(): pl.pallas_call(kernel, out_shape=(jax.ShapeDtypeStruct((KV, WIDTH), BF),...  61 us
    unnamed x2, local copies, waits for them, and re-layouts  1.67 us

profile of v3, /device:TPU:1, one launch (start us, length us, event | category | flops | bytes accessed | tf_op | source)
XLA Modules:
  0.0 63.3 jit_solution(7446111214426122286)
XLA Ops:
  0.6 61.0 %shard_map.113 = (bf16[512,640]{1,0:T(8,128)(2,1)S(1)}, bf16[1,512,640]{2,1,0:T(8,128)(2,1)S(1)}) custom-call(bf16[4,2,160,640]{3,2,1,0:T(8,128)(2,1)} %bitcast.3, bf16[512,640]{1,0:T(8,128)(2,1)} %w_hbm.1, f32[1,512]{1,0:T(1,128)} %bitcast.5, bf16[64,1280]{1,0:T(8,128)(2,1)} %bitcast.4, bf16[1,512,640]{2,1,0:T(8,128)(2,1)} %mom_hbm.1, s32[8,10]{1,0:T(8,128)} %row_hbm.1, ...), custom_call_target="tpu_custom_call" | custom-call | flops 2500000000 | bytes 6000000 | tf_op jit(solution)/shard_map/pallas_call | solution.py:354
  61.7 0.8 %copy.14 = bf16[512,640]{1,0:T(8,128)(2,1)} copy(bf16[512,640]{1,0:T(8,128)(2,1)S(1)} %get-tuple-element.4) | data formatting | bytes 1310720
  62.5 0.8 %copy.15 = bf16[1,512,640]{2,1,0:T(8,128)(2,1)} copy(bf16[1,512,640]{2,1,0:T(8,128)(2,1)S(1)} %get-tuple-element.5) | data formatting | bytes 1310720

commit v4 on v3

--- a/solution.py
+++ b/solution.py
@@ -30,6 +30,7 @@
 ROWS_BLK = KV // SPAN
 COLS_BLK = WIDTH // SPAN
 LANES = 128
+WINDOW = 3 * LANES
 CHUNKS = ((0, 80), (80, 80))
 WAYS = ((1, slice(0, 256)), (3, slice(256, 512)))
 
@@ -69,7 +70,7 @@
     x_hbm, w_hbm, gain_hbm, cot_hbm, mom_hbm, row_hbm, col_hbm, left_hbm, left_t_hbm, right_hbm,
     upd_v, new_v,
     xv, wv, gain_ref, row_ref, col_ref, momv, left_f, left_t_f, right_f, leftv, left_tv, rightv,
-    cot_pair, cot_mix, cot_all, part_out, part_own, part_in, pair, relay, relay_sum, recv, dk, mom_new,
+    cot_in, cot_t, part_out, part_own, part_in, pair, relay, relay_sum, recv, dk, mom_new,
     row_mask, col_mask, band_y, band_xz,
     load_sem, cs_s, cs_r, cz_s, cz_r, ps_s, ps_r, r1_s, r1_r, rd_s, rd_r, r2_s, r2_r, ag_s, ag_r, a2_s, a2_r, fw_s, fw_r,
     y_s, y_r, xz_s, xz_r,
@@ -105,7 +106,7 @@
         at = (slice(None), slice(None), pl.ds(off, rows))
         loads.append(pltpu.make_async_copy(x_hbm.at[at], xv.at[at], load_sem.at[1 + k]))
     base = 1 + len(CHUNKS)
-    more = [(cot_hbm, cot_pair.at[core]), (gain_hbm, gain_ref), (row_hbm, row_ref), (col_hbm, col_ref), (mom_hbm, momv)]
+    more = [(cot_hbm.at[:, pl.ds(pl.multiple_of((zh * 5 // 2) * LANES, LANES), WINDOW)], cot_in.at[zh, core]), (gain_hbm, gain_ref), (row_hbm, row_ref), (col_hbm, col_ref), (mom_hbm, momv)]
     more += [(left_hbm, left_f), (left_t_hbm, left_t_f), (right_hbm, right_f)]
     for k, (src, dst) in enumerate(more):
         loads.append(pltpu.make_async_copy(src, dst, load_sem.at[base + k]))
@@ -115,6 +116,9 @@
     for load in loads[base + 1 :]:
         load.start()
 
+    def window(chip):
+        return pl.ds(pl.multiple_of((chip * 5 // 2) * LANES, LANES), WINDOW)
+
     def remote(src, dst, send, recv_, peer):
         return pltpu.make_async_remote_copy(
             src_ref=src, dst_ref=dst, send_sem=send, recv_sem=recv_, device_id=peer, device_id_type=MESH
@@ -152,11 +156,13 @@
     for k in range(len(CHUNKS)):
         partial_keys(k)
     pl.semaphore_wait(barrier, len(near) + len(far))
+    for step in (2, 1, 3):
+        start(("cz", step), remote(
+            cot_hbm.at[:, window((zh + step) % NZ)], cot_in.at[zh, core],
+            cz_s.at[step - 1], cz_r.at[step - 1], z_peer(step),
+        ))
     for k in range(len(CHUNKS)):
         swap_parts(k)
-    cot_swap = remote(cot_hbm, cot_pair.at[core], cs_s, cs_r, sib)
-    start(("cs",), cot_swap)
-
     for k, (off, rows) in enumerate(CHUNKS):
         at = pl.ds(off, rows)
         landed(("ps", k), part_swaps[k])
@@ -166,14 +172,6 @@
                 pair.at[(zh + 2) % NZ, at, half], relay.at[way, at], r1_s.at[k, way], r1_r.at[k, way], z_peer(step)
             ))
 
-    loads[base].wait()
-    landed(("cs",), cot_swap)
-    cot_mix[...] = cot_pair[...].reshape(LANES, 2 * NZ * OWN).T.reshape(NZ, 2, OWN, LANES)
-    cot_all[zh] = cot_mix[zh, core]
-    for step in (2, 1, 3):
-        start(("cz", step), remote(
-            cot_mix.at[(zh + step) % NZ, core], cot_all.at[zh], cz_s.at[step - 1], cz_r.at[step - 1], z_peer(step)
-        ))
     for k, (off, rows) in enumerate(CHUNKS):
         at = pl.ds(off, rows)
         for way, (step, half) in enumerate(WAYS):
@@ -218,9 +216,16 @@
         for part in range(2):
             rightv[part, c * SPAN : (c + 1) * SPAN] = jnp.where(lane_block == c, right_f[part], 0.0).astype(BF)
 
-    for step in (2, 1, 3):
+    loads[base].wait()
+    for step in (1, 3, 2):
         src = (zh + NZ - step) % NZ
-        landed(("cz", step), remote(cot_mix.at[0, 0], cot_all.at[src], cz_s.at[step - 1], cz_r.at[step - 1], sib))
+        landed(("cz", step), remote(
+            cot_hbm.at[:, pl.ds(0, WINDOW)], cot_in.at[src, core], cz_s.at[step - 1], cz_r.at[step - 1], sib
+        ))
+    start(("cs",), remote(cot_in.at[:, core], cot_in.at[:, core], cs_s, cs_r, sib))
+    landed(("cs",), remote(cot_in.at[:, 1 - core], cot_in.at[:, 1 - core], cs_s, cs_r, sib))
+    cot_t[...] = cot_in[...].reshape(KV, WINDOW).T.astype(F32)
+    cot_base = pl.multiple_of((zh % 2) * 64 + core * OWN, 32)
     gain = gain_ref[...]
     for k, (off, rows) in enumerate(CHUNKS):
         at = pl.ds(off, rows)
@@ -234,7 +239,7 @@
                 relay_sum.at[way, at], recv.at[way, at, half], r2_s.at[k, way], r2_r.at[k, way], sib
             ))
         keys = pair[zh, at, :].astype(F32) + recv[0, at, :].astype(F32) + recv[1, at, :].astype(F32)
-        scaled = gain * jnp.concatenate([cot_all[j, at, :].astype(F32) for j in range(NZ)], axis=-1)
+        scaled = gain * cot_t[pl.ds(cot_base + off, rows), :]
         inverse = lax.rsqrt(jnp.mean(keys * keys, axis=-1, keepdims=True) + EPS)
         inner = jnp.sum(scaled * keys, axis=-1, keepdims=True)
         dk[mp, at, :] = (inverse * scaled - (inverse * inverse * inverse * inner / KV) * keys).astype(BF)
@@ -372,9 +377,8 @@
             pltpu.VMEM(left.shape, BF),
             pltpu.VMEM(left_t.shape, BF),
             pltpu.VMEM((2, WIDTH, OFFSETS * LANES), BF),
-            pltpu.VMEM((2, SPAN, 2 * NZ * OWN), BF),
-            pltpu.VMEM((NZ, 2, OWN, LANES), BF),
-            pltpu.VMEM((NZ, OWN, LANES), BF),
+            pltpu.VMEM((NZ, 2, KV // (2 * NZ), WINDOW), BF),
+            pltpu.VMEM((WINDOW, KV), F32),
             pltpu.VMEM((NZ, OWN, KV), BF),
             pltpu.VMEM((NZ, OWN, KV), BF),
             pltpu.VMEM((NZ, OWN, KV), BF),

time: 63.5 us -> 62 us (0.976)
  Pallas kernels: 61 us -> 59.5 us
    pallas_call x1, Pallas kernels: 61 us -> 59.5 us  [on_device(): pl.pallas_call(kernel, out_shape=(jax.ShapeDtypeStruct((KV, WIDTH), BF),...]
where the time goes in v4:
time: 62 us; the launch traced here: 61.9 us
  Pallas kernels  59.5 us (96%)
  local copies, waits for them, and re-layouts  1.67 us (3%)
  between operations  0.64 us (1%)
    pallas_call x1, Pallas kernels, on_device(): pl.pallas_call(kernel, out_shape=(jax.ShapeDtypeStruct((KV, WIDTH), BF),...  59.5 us
    unnamed x2, local copies, waits for them, and re-layouts  1.67 us

profile of v4, /device:TPU:1, one launch (start us, length us, event | category | flops | bytes accessed | tf_op | source)
XLA Modules:
  0.0 61.9 jit_solution(14538564115121320732)
XLA Ops:
  0.6 59.5 %shard_map.113 = (bf16[512,640]{1,0:T(8,128)(2,1)S(1)}, bf16[1,512,640]{2,1,0:T(8,128)(2,1)S(1)}) custom-call(bf16[4,2,160,640]{3,2,1,0:T(8,128)(2,1)} %bitcast.3, bf16[512,640]{1,0:T(8,128)(2,1)} %w_hbm.1, f32[1,512]{1,0:T(1,128)} %bitcast.5, bf16[64,1280]{1,0:T(8,128)(2,1)} %bitcast.4, bf16[1,512,640]{2,1,0:T(8,128)(2,1)} %mom_hbm.1, s32[8,10]{1,0:T(8,128)} %row_hbm.1, ...), custom_call_target="tpu_custom_call" | custom-call | flops 2500000000 | bytes 6000000 | tf_op jit(solution)/shard_map/pallas_call | solution.py:359
  60.2 0.8 %copy.14 = bf16[512,640]{1,0:T(8,128)(2,1)} copy(bf16[512,640]{1,0:T(8,128)(2,1)S(1)} %get-tuple-element.4) | data formatting | bytes 1310720
  61.0 0.8 %copy.15 = bf16[1,512,640]{2,1,0:T(8,128)(2,1)} copy(bf16[1,512,640]{2,1,0:T(8,128)(2,1)S(1)} %get-tuple-element.5) | data formatting | bytes 1310720

commit v5 on v4

--- a/solution.py
+++ b/solution.py
@@ -31,7 +31,8 @@
 COLS_BLK = WIDTH // SPAN
 LANES = 128
 WINDOW = 3 * LANES
-CHUNKS = ((0, 80), (80, 80))
+CHUNKS = ((0, 64), (64, 96))
+FEATURES = (slice(0, 32), slice(32, 64))
 WAYS = ((1, slice(0, 256)), (3, slice(256, 512)))
 
 
@@ -70,10 +71,10 @@
     x_hbm, w_hbm, gain_hbm, cot_hbm, mom_hbm, row_hbm, col_hbm, left_hbm, left_t_hbm, right_hbm,
     upd_v, new_v,
     xv, wv, gain_ref, row_ref, col_ref, momv, left_f, left_t_f, right_f, leftv, left_tv, rightv,
-    cot_in, cot_t, part_out, part_own, part_in, pair, relay, relay_sum, recv, dk, mom_new,
+    cot_in, cot_relay, cot_t, part_out, part_own, part_in, pair, relay, relay_sum, recv, dk, mom_new, sections,
     row_mask, col_mask, band_y, band_xz,
-    load_sem, cs_s, cs_r, cz_s, cz_r, ps_s, ps_r, r1_s, r1_r, rd_s, rd_r, r2_s, r2_r, ag_s, ag_r, a2_s, a2_r, fw_s, fw_r,
-    y_s, y_r, xz_s, xz_r,
+    load_sem, cs_s, cs_r, cr_s, cr_r, cf_s, cf_r, cz_s, cz_r, ps_s, ps_r, r1_s, r1_r, rd_s, rd_r, r2_s, r2_r, ag_s, ag_r, a2_s, a2_r, fw_s, fw_r,
+    y_s, y_r, xz_s, xz_r, heard,
 ):
     dp = lax.axis_index("dp")
     mp = lax.axis_index("mp")
@@ -93,8 +94,12 @@
         return {"dp": ((xz + step) % NXZ) * NY + y, "mp": mp}
 
     barrier = pltpu.get_barrier_semaphore()
-    near = [z_peer(s) for s in (2, 1, 3)] + [sib]
-    far = [y_peer(s) for s in (4, 3, 5, 2, 6, 1, 7)] + [xz_peer(s) for s in range(1, NXZ)]
+    def x_peer(step, flip):
+        return {"dp": (((xz // 2 + step) % (NXZ // 2)) * 2 + (xz % 2 + flip) % 2) * NY + y, "mp": mp}
+
+    near = [z_peer(1), z_peer(3), sib]
+    far = [y_peer(s) for s in (2, 6, 1, 7)]
+    far += [x_peer(2, 0), x_peer(1, 1), x_peer(3, 1), x_peer(1, 0), x_peer(3, 0), x_peer(0, 1)]
 
     def greet(peers):
         for peer in peers:
@@ -153,16 +158,24 @@
         start(("ps", k), part_swaps[k])
 
     loads[0].wait()
-    for k in range(len(CHUNKS)):
+    partial_keys(0)
+    pl.semaphore_wait(barrier, len(near) + len(far))
+    for way, (step, half) in enumerate(WAYS):
+        start(("cr", way), remote(
+            cot_hbm.at[FEATURES[way], window((zh + 2) % NZ)], cot_relay.at[way], cr_s.at[way], cr_r.at[way], z_peer(step)
+        ))
+    for way, (step, half) in enumerate(WAYS):
+        start(("cz", way), remote(
+            cot_hbm.at[:, window((zh + step) % NZ)], cot_in.at[zh, core], cz_s.at[way], cz_r.at[way], z_peer(step)
+        ))
+    swap_parts(0)
+    for k in range(1, len(CHUNKS)):
         partial_keys(k)
-    pl.semaphore_wait(barrier, len(near) + len(far))
-    for step in (2, 1, 3):
-        start(("cz", step), remote(
-            cot_hbm.at[:, window((zh + step) % NZ)], cot_in.at[zh, core],
-            cz_s.at[step - 1], cz_r.at[step - 1], z_peer(step),
-        ))
-    for k in range(len(CHUNKS)):
         swap_parts(k)
+    heralds = [y_peer(2), y_peer(6), x_peer(2, 0)]
+    for peer in heralds:
+        pl.semaphore_signal(heard, inc=1, device_id=peer, device_id_type=MESH)
+
     for k, (off, rows) in enumerate(CHUNKS):
         at = pl.ds(off, rows)
         landed(("ps", k), part_swaps[k])
@@ -180,6 +193,16 @@
                 pair.at[(zh + step) % NZ, at, other], recv.at[way, at, other],
                 rd_s.at[k, way], rd_r.at[k, way], z_peer(step),
             ))
+    for load in loads[base + 1 :]:
+        load.wait()
+    mom_new[...] = DECAY * momv[0].astype(F32)
+    leftv[...] = left_f[...].astype(BF)
+    left_tv[...] = left_t_f[...].astype(BF)
+    for way, (step, half) in enumerate(WAYS):
+        landed(("cr", way), remote(cot_relay.at[way], cot_relay.at[way], cr_s.at[way], cr_r.at[way], sib))
+        start(("cf", way), remote(
+            cot_relay.at[way], cot_in.at[(zh + NZ - step) % NZ, core, FEATURES[way]], cf_s.at[way], cf_r.at[way], z_peer(step)
+        ))
     for k, (off, rows) in enumerate(CHUNKS):
         at = pl.ds(off, rows)
         for way, (step, half) in enumerate(WAYS):
@@ -205,23 +228,13 @@
         col_mask[r] = of_col
         return carry
 
-    for load in loads[base + 1 :]:
-        load.wait()
     lax.fori_loop(0, ROWS_BLK, spread, 0)
-    mom_new[...] = DECAY * momv[0].astype(F32)
-    leftv[...] = left_f[...].astype(BF)
-    left_tv[...] = left_t_f[...].astype(BF)
-    lane_block = (lax.broadcasted_iota(jnp.int32, (SPAN, OFFSETS * LANES), 1) % LANES) // BAND
-    for c in range(COLS_BLK):
-        for part in range(2):
-            rightv[part, c * SPAN : (c + 1) * SPAN] = jnp.where(lane_block == c, right_f[part], 0.0).astype(BF)
-
     loads[base].wait()
-    for step in (1, 3, 2):
-        src = (zh + NZ - step) % NZ
-        landed(("cz", step), remote(
-            cot_hbm.at[:, pl.ds(0, WINDOW)], cot_in.at[src, core], cz_s.at[step - 1], cz_r.at[step - 1], sib
-        ))
+    for way, (step, half) in enumerate(WAYS):
+        got = cot_in.at[(zh + NZ - step) % NZ, core]
+        landed(("cz", way), remote(got, got, cz_s.at[way], cz_r.at[way], sib))
+        got = cot_in.at[(zh + 2) % NZ, core, FEATURES[way]]
+        landed(("cf", way), remote(got, got, cf_s.at[way], cf_r.at[way], sib))
     start(("cs",), remote(cot_in.at[:, core], cot_in.at[:, core], cs_s, cs_r, sib))
     landed(("cs",), remote(cot_in.at[:, 1 - core], cot_in.at[:, 1 - core], cs_s, cs_r, sib))
     cot_t[...] = cot_in[...].reshape(KV, WINDOW).T.astype(F32)
@@ -248,6 +261,11 @@
             start(("ag", k, way), remote(mine, mine, ag_s.at[k, way], ag_r.at[k, way], z_peer(step)))
         start(("fw", k, 0), remote(mine, mine, fw_s.at[k, 0], fw_r.at[k, 0], sib))
 
+    lane_block = (lax.broadcasted_iota(jnp.int32, (SPAN, OFFSETS * LANES), 1) % LANES) // BAND
+    for c in range(COLS_BLK):
+        for part in range(2):
+            rightv[part, c * SPAN : (c + 1) * SPAN] = jnp.where(lane_block == c, right_f[part], 0.0).astype(BF)
+
     def owner(step, side):
         return ((zh + NZ - step) % NZ) * 2 + side
 
@@ -259,6 +277,23 @@
             part = dk.at[owner(step, core), at, half]
             start(("a2", k, way), remote(part, part, a2_s.at[k, way], a2_r.at[k, way], z_peer(step)))
             start(("fw", k, step), remote(got, got, fw_s.at[k, step], fw_r.at[k, step], sib))
+    def wait_other_core(k, step):
+        got = dk.at[owner(step, 1 - core), pl.ds(*CHUNKS[k])]
+        landed(("fw", k, step), remote(got, got, fw_s.at[k, step], fw_r.at[k, step], sib))
+
+    def part_gradient(k, steps):
+        off, rows = CHUNKS[k]
+        chips = [(zh + NZ - step) % NZ for step in steps]
+        some_dk = [dk[pl.ds(2 * chip, 2), pl.ds(off, rows), :].reshape(2 * rows, KV) for chip in chips]
+        some_x = [xv[chip, :, pl.ds(off, rows), :].reshape(2 * rows, WIDTH) for chip in chips]
+        some_dk, some_x = jnp.concatenate(some_dk, axis=0), jnp.concatenate(some_x, axis=0)
+        return dot(some_dk, some_x, ((0,), (0,))) * (1.0 / math.sqrt(2 * NZ * OWN))
+
+    last = len(CHUNKS) - 1
+    for k in range(len(CHUNKS)):
+        for step in (0, 1, 3):
+            wait_other_core(k, step)
+        mom_new[...] += part_gradient(k, (0, 1, 3))
     for k, (off, rows) in enumerate(CHUNKS):
         at = pl.ds(off, rows)
         for way, (step, half) in enumerate(WAYS):
@@ -266,19 +301,20 @@
             landed(("a2", k, way), remote(part, part, a2_s.at[k, way], a2_r.at[k, way], sib))
         got = dk.at[owner(2, core), at]
         start(("fw", k, 2), remote(got, got, fw_s.at[k, 2], fw_r.at[k, 2], sib))
-        for step in (0, 1, 3, 2):
-            got = dk.at[owner(step, 1 - core), at]
-            landed(("fw", k, step), remote(got, got, fw_s.at[k, step], fw_r.at[k, step], sib))
-        all_dk = dk[:, at, :].reshape(2 * NZ * rows, KV)
-        all_x = xv[:, :, at, :].reshape(2 * NZ * rows, WIDTH)
-        mom_new[...] += dot(all_dk, all_x, ((0,), (0,))) * (1.0 / math.sqrt(2 * NZ * OWN))
+        if k == last:
+            for g in range(2):
+                high, low = split(mom_new[g * 256 : (g + 1) * 256, :])
+                both = dot(leftv[...], high)
+                sections[g] = both[:128] + both[128:] + dot(leftv[:128], low)
+        wait_other_core(k, 2)
+        if k < last:
+            mom_new[...] += part_gradient(k, (2,))
+    last_piece = part_gradient(last, (2,))
 
     picked = []
     for g in range(2):
-        high, low = split(mom_new[g * 256 : (g + 1) * 256, :])
-        both = dot(leftv[...], high)
-        sect = both[:128] + both[128:] + dot(leftv[:128], low)
-        sect = sect.reshape(4, OFFSETS, BAND, WIDTH)
+        both = dot(leftv[...], last_piece[g * 256 : (g + 1) * 256].astype(BF))
+        sect = (sections[g] + both[:128] + both[128:]).reshape(4, OFFSETS, BAND, WIDTH)
         chosen = row_mask[g * 4 : (g + 1) * 4]
         total = jnp.zeros((4, BAND, WIDTH), F32)
         for band in range(OFFSETS):
@@ -294,9 +330,11 @@
         coeffs = coeffs + jnp.where(chosen == band, full[:, band * LANES : (band + 1) * LANES], 0.0)
 
     band_y[y] = coeffs.astype(BF)
+    pl.semaphore_wait(heard, len(heralds))
     for step in (4, 3, 5, 2, 6, 1, 7):
         start(("y", step), remote(band_y.at[y], band_y.at[y], y_s.at[step - 1], y_r.at[step - 1], y_peer(step)))
 
+    mom_new[...] += last_piece
     def rebuild(values, exact, put):
         parts = [jnp.where(chosen == band, values, 0.0) for band in range(OFFSETS)]
         high, low = split(jnp.concatenate(parts, axis=1))
@@ -378,6 +416,7 @@
             pltpu.VMEM(left_t.shape, BF),
             pltpu.VMEM((2, WIDTH, OFFSETS * LANES), BF),
             pltpu.VMEM((NZ, 2, KV // (2 * NZ), WINDOW), BF),
+            pltpu.VMEM((2, KV // (4 * NZ), WINDOW), BF),
             pltpu.VMEM((WINDOW, KV), F32),
             pltpu.VMEM((NZ, OWN, KV), BF),
             pltpu.VMEM((NZ, OWN, KV), BF),
@@ -388,6 +427,7 @@
             pltpu.VMEM((2, OWN, KV), BF),
             pltpu.VMEM((2 * NZ, OWN, KV), BF),
             pltpu.VMEM((KV, WIDTH), F32),
+            pltpu.VMEM((2, 128, WIDTH), F32),
             pltpu.VMEM((ROWS_BLK, BAND, WIDTH), jnp.int32),
             pltpu.VMEM((ROWS_BLK, BAND, LANES), jnp.int32),
             pltpu.VMEM((NY, 64, LANES), BF),
@@ -395,8 +435,12 @@
             dma((9 + n,)),
             dma(()),
             dma(()),
-            dma((3,)),
-            dma((3,)),
+            dma((2,)),
+            dma((2,)),
+            dma((2,)),
+            dma((2,)),
+            dma((2,)),
+            dma((2,)),
             dma((n,)),
             dma((n,)),
             dma((n, 2)),
@@ -415,6 +459,7 @@
             dma((7,)),
             dma((7,)),
             dma((7,)),
+            pltpu.SemaphoreType.REGULAR,
         ],
         compiler_params=pltpu.CompilerParams(
             collective_id=0, has_side_effects=True, vmem_limit_bytes=48 * 1024 * 1024

time: 62 us -> 61.2 us (0.987)
  Pallas kernels: 59.5 us -> 58.8 us
    pallas_call x1, Pallas kernels: 59.5 us -> 58.8 us  [on_device(): pl.pallas_call(kernel, out_shape=(jax.ShapeDtypeStruct((KV, WIDTH), BF),...]
where the time goes in v5:
time: 61.2 us; the launch traced here: 61.1 us
  Pallas kernels  58.8 us (96%)
  local copies, waits for them, and re-layouts  1.67 us (3%)
  between operations  0.64 us (1%)
    pallas_call x1, Pallas kernels, on_device(): pl.pallas_call(kernel, out_shape=(jax.ShapeDtypeStruct((KV, WIDTH), BF),...  58.8 us
    unnamed x2, local copies, waits for them, and re-layouts  1.67 us

profile of v5, /device:TPU:1, one launch (start us, length us, event | category | flops | bytes accessed | tf_op | source)
XLA Modules:
  0.0 61.1 jit_solution(2490710513746574551)
XLA Ops:
  0.6 58.8 %shard_map.113 = (bf16[512,640]{1,0:T(8,128)(2,1)S(1)}, bf16[1,512,640]{2,1,0:T(8,128)(2,1)S(1)}) custom-call(bf16[4,2,160,640]{3,2,1,0:T(8,128)(2,1)} %bitcast.3, bf16[512,640]{1,0:T(8,128)(2,1)} %w_hbm.1, f32[1,512]{1,0:T(1,128)} %bitcast.5, bf16[64,1280]{1,0:T(8,128)(2,1)} %bitcast.4, bf16[1,512,640]{2,1,0:T(8,128)(2,1)} %mom_hbm.1, s32[8,10]{1,0:T(8,128)} %row_hbm.1, ...), custom_call_target="tpu_custom_call" | custom-call | flops 2500000000 | bytes 6000000 | tf_op jit(solution)/shard_map/pallas_call | solution.py:397
  59.4 0.8 %copy.14 = bf16[512,640]{1,0:T(8,128)(2,1)} copy(bf16[512,640]{1,0:T(8,128)(2,1)S(1)} %get-tuple-element.4) | data formatting | bytes 1310720
  60.3 0.8 %copy.15 = bf16[1,512,640]{2,1,0:T(8,128)(2,1)} copy(bf16[1,512,640]{2,1,0:T(8,128)(2,1)S(1)} %get-tuple-element.5) | data formatting | bytes 1310720

commit v6 on v5

--- a/solution.py
+++ b/solution.py
@@ -31,7 +31,7 @@
 COLS_BLK = WIDTH // SPAN
 LANES = 128
 WINDOW = 3 * LANES
-CHUNKS = ((0, 64), (64, 96))
+CHUNKS = ((0, 48), (48, 112))
 FEATURES = (slice(0, 32), slice(32, 64))
 WAYS = ((1, slice(0, 256)), (3, slice(256, 512)))
 

time: 61.2 us -> 60.3 us (0.985)
  Pallas kernels: 58.8 us -> 57.5 us
    pallas_call x1, Pallas kernels: 58.8 us -> 57.5 us  [on_device(): pl.pallas_call(kernel, out_shape=(jax.ShapeDtypeStruct((KV, WIDTH), BF),...]
where the time goes in v6:
time: 60.3 us; the launch traced here: 59.9 us
  Pallas kernels  57.5 us (95%)
  local copies, waits for them, and re-layouts  1.67 us (3%)
  between operations  0.64 us (1%)
    pallas_call x1, Pallas kernels, on_device(): pl.pallas_call(kernel, out_shape=(jax.ShapeDtypeStruct((KV, WIDTH), BF),...  57.5 us
    unnamed x2, local copies, waits for them, and re-layouts  1.67 us

profile of v6, /device:TPU:1, one launch (start us, length us, event | category | flops | bytes accessed | tf_op | source)
XLA Modules:
  0.0 59.9 jit_solution(15818347003382866794)
XLA Ops:
  0.6 57.5 %shard_map.113 = (bf16[512,640]{1,0:T(8,128)(2,1)S(1)}, bf16[1,512,640]{2,1,0:T(8,128)(2,1)S(1)}) custom-call(bf16[4,2,160,640]{3,2,1,0:T(8,128)(2,1)} %bitcast.3, bf16[512,640]{1,0:T(8,128)(2,1)} %w_hbm.1, f32[1,512]{1,0:T(1,128)} %bitcast.5, bf16[64,1280]{1,0:T(8,128)(2,1)} %bitcast.4, bf16[1,512,640]{2,1,0:T(8,128)(2,1)} %mom_hbm.1, s32[8,10]{1,0:T(8,128)} %row_hbm.1, ...), custom_call_target="tpu_custom_call" | custom-call | flops 2500000000 | bytes 6000000 | tf_op jit(solution)/shard_map/pallas_call | solution.py:397
  58.2 0.8 %copy.14 = bf16[512,640]{1,0:T(8,128)(2,1)} copy(bf16[512,640]{1,0:T(8,128)(2,1)S(1)} %get-tuple-element.4) | data formatting | bytes 1310720
  59.0 0.8 %copy.15 = bf16[1,512,640]{2,1,0:T(8,128)(2,1)} copy(bf16[1,512,640]{2,1,0:T(8,128)(2,1)S(1)} %get-tuple-element.5) | data formatting | bytes 1310720

commit v7 on v6

--- a/solution.py
+++ b/solution.py
@@ -143,11 +143,10 @@
 
     part_swaps = []
 
-    def partial_keys(k):
+    def partial_keys(k, halves):
         off, rows = CHUNKS[k]
-        loads[1 + k].wait()
-        at = pl.ds(off, rows)
-        for side, place in ((1 - core, part_out), (core, part_own)):
+        at = pl.ds(off, rows)
+        for side, place in halves:
             x_rows = xv[:, side, at, :].reshape(NZ * rows, WIDTH)
             part = dot(x_rows, wv[...], ((1,), (1,)))
             place[:, at, :] = part.astype(BF).reshape(NZ, rows, KV)
@@ -158,7 +157,9 @@
         start(("ps", k), part_swaps[k])
 
     loads[0].wait()
-    partial_keys(0)
+    away, stay = (1 - core, part_out), (core, part_own)
+    loads[1].wait()
+    partial_keys(0, (away, stay))
     pl.semaphore_wait(barrier, len(near) + len(far))
     for way, (step, half) in enumerate(WAYS):
         start(("cr", way), remote(
@@ -170,7 +171,8 @@
         ))
     swap_parts(0)
     for k in range(1, len(CHUNKS)):
-        partial_keys(k)
+        loads[1 + k].wait()
+        partial_keys(k, (away,))
         swap_parts(k)
     heralds = [y_peer(2), y_peer(6), x_peer(2, 0)]
     for peer in heralds:
@@ -178,6 +180,8 @@
 
     for k, (off, rows) in enumerate(CHUNKS):
         at = pl.ds(off, rows)
+        if k > 0:
+            partial_keys(k, (stay,))
         landed(("ps", k), part_swaps[k])
         pair[:, at, :] = (part_own[:, at, :].astype(F32) + part_in[:, at, :].astype(F32)).astype(BF)
         for way, (step, half) in enumerate(WAYS):
@@ -367,7 +371,7 @@
     for j in range(1, NY):
         total = total + band_y[j].astype(F32)
     band_xz[xz] = total.astype(BF)
-    for step in range(1, NXZ):
+    for step in (4, 3, 5, 2, 6, 1, 7):
         start(("xz", step), remote(band_xz.at[xz], band_xz.at[xz], xz_s.at[step - 1], xz_r.at[step - 1], xz_peer(step)))
     for step in range(1, NXZ):
         got = band_xz.at[(xz + NXZ - step) % NXZ]

time: 60.3 us -> 60.2 us (level)
  no operation moved by 1% of the time
where the time goes in v7:
time: 60.2 us; the launch traced here: 60 us
  Pallas kernels  57.7 us (96%)
  local copies, waits for them, and re-layouts  1.67 us (3%)
  between operations  0.64 us (1%)
    pallas_call x1, Pallas kernels, on_device(): pl.pallas_call(kernel, out_shape=(jax.ShapeDtypeStruct((KV, WIDTH), BF),...  57.7 us
    unnamed x2, local copies, waits for them, and re-layouts  1.67 us

profile of v7, /device:TPU:1, one launch (start us, length us, event | category | flops | bytes accessed | tf_op | source)
XLA Modules:
  0.0 60.0 jit_solution(10466950839817799625)
XLA Ops:
  0.6 57.7 %shard_map.113 = (bf16[512,640]{1,0:T(8,128)(2,1)S(1)}, bf16[1,512,640]{2,1,0:T(8,128)(2,1)S(1)}) custom-call(bf16[4,2,160,640]{3,2,1,0:T(8,128)(2,1)} %bitcast.3, bf16[512,640]{1,0:T(8,128)(2,1)} %w_hbm.1, f32[1,512]{1,0:T(1,128)} %bitcast.5, bf16[64,1280]{1,0:T(8,128)(2,1)} %bitcast.4, bf16[1,512,640]{2,1,0:T(8,128)(2,1)} %mom_hbm.1, s32[8,10]{1,0:T(8,128)} %row_hbm.1, ...), custom_call_target="tpu_custom_call" | custom-call | flops 2500000000 | bytes 6000000 | tf_op jit(solution)/shard_map/pallas_call | solution.py:401
  58.4 0.8 %copy.14 = bf16[512,640]{1,0:T(8,128)(2,1)} copy(bf16[512,640]{1,0:T(8,128)(2,1)S(1)} %get-tuple-element.4) | data formatting | bytes 1310720
  59.2 0.8 %copy.15 = bf16[1,512,640]{2,1,0:T(8,128)(2,1)} copy(bf16[1,512,640]{2,1,0:T(8,128)(2,1)S(1)} %get-tuple-element.5) | data formatting | bytes 1310720
